TPU v7x, 32 devices: a whole 2x2x4 slice. The times are simulated.
32 devices in a mesh: row: 4 (over y, core), col: 2 (over x), blk: 4 (over z).
Axes of the slice: x: 2, y: 2, z: 4, core: 2. Of those that a mesh axis runs over, the one named last changes fastest.
Arguments:
- pixels: bfloat16 [256, 64, 1024], P('row', 'col', 'blk'), may hold values from -6 to 6
- dw_kernel: float32 [7, 7, 1024], P(None, None, 'blk'), may hold values from -4 to 4
- dw_bias: float32 [1024], P('blk'), may hold values from -3 to 3
- ln_gain: float32 [1024], P('blk'), may hold values from 0.25 to 1.75
- ln_bias: float32 [1024], P('blk'), may hold values from -2 to 2
- w_in: bfloat16 [4096, 1024], P('blk'), may hold values from -0.1875 to 0.1875
- b_in: bfloat16 [4096], P('blk'), may hold values from -2 to 2
- w_out: bfloat16 [4096, 1024], P('blk'), may hold values from -0.125 to 0.125
- b_out: float32 [1024], P('blk'), may hold values from -2 to 2
- layer_scale: float32 [1024], P('blk'), may hold values from 0.5 to 2
Outputs:
- block_out: bfloat16 [256, 64, 1024], P('row', 'col', 'blk')
All inputs are finite; a program needn't handle non-finite values.
Results may differ from a plain program's by a relative error of at most 0.012.
Values may be sent and summed in bfloat16 or wider, within the bound.
A program may use at most 64 MiB of HBM per device.

v0:
```python
import jax
import jax.numpy as jnp
from jax import lax
from jax.sharding import PartitionSpec as P

C = 1024
KS = 7


def with_halo(cells, sides, width):
    for axis, dim in sides:
        count = lax.axis_size(axis)
        ends = count - 1
        head = lax.slice_in_dim(cells, 0, width, axis=dim)
        tail = lax.slice_in_dim(cells, cells.shape[dim] - width, cells.shape[dim], axis=dim)
        cells = jnp.concatenate(
            [
                lax.ppermute(tail, axis, [(i, (i + 1) % count) for i in range(ends)]),
                cells,
                lax.ppermute(head, axis, [((i + 1) % count, i) for i in range(ends)]),
            ],
            axis=dim,
        )
    return cells


def shard_terms(rows, w_first, w_second, b_first):
    pre_act = jnp.einsum("tc,khc->kth", rows, w_first, preferred_element_type=jnp.float32)
    pre_act = pre_act + b_first[:, None, :].astype(jnp.float32)
    hidden = jax.nn.gelu(pre_act, approximate=False).astype(jnp.bfloat16)
    partial_value = jnp.einsum(
        "kth,khc->ktc", hidden, w_second, preferred_element_type=jnp.float32
    ).astype(jnp.bfloat16)
    partial_value = lax.optimization_barrier(partial_value)
    return jnp.sum(partial_value.astype(jnp.float32), axis=0)


def shards(pixels, dw_kernel, dw_bias, ln_gain, ln_bias, w_in, b_in, w_out, b_out, layer_scale):
    tile_rows, tile_cols, chans = pixels.shape
    reach = (KS - 1) // 2
    padded = with_halo(pixels, (("row", 0), ("col", 1)), reach).astype(jnp.float32)
    conv_out = jnp.zeros((tile_rows, tile_cols, chans), jnp.float32) + dw_bias
    for row_off in range(KS):
        for col_off in range(KS):
            conv_out = (
                conv_out
                + padded[row_off : row_off + tile_rows, col_off : col_off + tile_cols, :]
                * dw_kernel[row_off, col_off]
            )
    first_sum = lax.psum(jnp.sum(conv_out, axis=-1), "blk")
    centred = conv_out - (first_sum / C)[..., None]
    spread = lax.psum(jnp.sum(centred * centred, axis=-1), "blk") / C
    normed = (centred * lax.rsqrt(spread + 1e-06)[..., None] * ln_gain + ln_bias).astype(
        jnp.bfloat16
    )
    pixel_count = tile_rows * tile_cols
    flat_rows = normed.reshape(pixel_count, chans)
    shard = w_in.shape[0]
    regrouped = lax.all_to_all(flat_rows, "blk", split_axis=0, concat_axis=1, tiled=True)
    w_first = lax.all_gather(w_in, "blk", axis=0, tiled=True)
    w_second = lax.all_gather(w_out, "blk", axis=0, tiled=True)
    b_first = lax.all_gather(b_in, "blk", axis=0, tiled=True)
    count = w_first.shape[0] // shard
    row_sums = shard_terms(
        regrouped,
        w_first.reshape(count, shard, C),
        w_second.reshape(count, shard, C),
        b_first.reshape(count, shard),
    )
    summed = lax.all_to_all(
        row_sums.astype(jnp.bfloat16), "blk", split_axis=1, concat_axis=0, tiled=True
    ).astype(row_sums.dtype)
    result = pixels.astype(jnp.float32) + layer_scale * (
        summed.reshape(tile_rows, tile_cols, chans) + b_out
    )
    return result.astype(jnp.bfloat16)


def solution(mesh):
    placed = (
        P("row", "col", "blk"),
        P(None, None, "blk"),
        P("blk"),
        P("blk"),
        P("blk"),
        P("blk", None),
        P("blk"),
        P("blk", None),
        P("blk"),
        P("blk"),
    )
    return jax.shard_map(
        shards, mesh=mesh, in_specs=placed, out_specs=P("row", "col", "blk"), check_vma=False
    )
```

profile of v0, /device:TPU:0, one launch (start us, length us, event | category | flops | bytes accessed | tf_op | source)
XLA Modules:
  0.0 408.3 jit_solution(17140278420504043308)
XLA Ops:
  6.5 0.7 all-gather.3.cloned.1.call-update
  7.3 0.7 all-gather.5.cloned.1.call-update
  8.0 1.3 collective-permute-start.1
  9.3 3.0 collective-permute-start
  12.4 0.6 fusion.140
  13.0 0.2 collective-permute-done
  13.2 0.1 constant_dynamic-update-slice_fusion.1
  13.3 0.1 fusion.137
  13.5 4.9 %collective-permute-start.2 = (bf16[70,3,256]{2,1,0:T(4,128)(2,1)S(1)}, bf16[70,3,256]{2,1,0:T(4,128)(2,1)S(1)}, u32[]{:S(2)}, u32[]{:S(2)}) collective-permute-start(bf16[70,3,256]{2,1,0:T(4,128)(2,1)S(1)} %get-tuple-element.7), channel_id=1, source_target_pairs={{0,4},{1,5},{2,6},{3,7},{8,12},{9,13},{10,14},{11,15},{16,20},{17,... | collective-permute-start | bytes 322568 | tf_op jit(solution)/shard_map/ppermute | solution.py:18
  18.3 1.3 collective-permute-start.3
  19.6 0.6 fusion.141
  20.3 1.8 collective-permute-done.2
  22.1 4.6 %collective-permute-done.3 = bf16[70,3,256]{2,1,0:T(4,128)(2,1)S(1)} collective-permute-done((bf16[70,3,256]{2,1,0:T(4,128)(2,1)S(1)}, bf16[70,3,256]{2,1,0:T(4,128)(2,1)S(1)}, u32[]{:S(2)}, u32[]{:S(2)}) %collective-permute-start.3) | collective-permute-done | bytes 107552 | tf_op jit(solution)/shard_map/ppermute | solution.py:20
  26.7 0.6 maximum_convert_fusion
  27.3 16.4 %fusion.135 = (f32[64,32]{1,0:T(8,128)S(1)}, f32[64,32,256]{2,1,0:T(8,128)S(1)}) fusion(f32[256]{0:T(256)} %bitcast.180, f32[70,38,256]{2,1,0:T(8,128)S(1)} %maximum_convert_fusion, f32[256]{0:T(256)} %bitcast.181, f32[256]{0:T(256)S(1)} %bitcast.134, f32[256]{0:T(256)S(1)} %bitcast.135, f32[256]{0:T(256)S(1)} %bitcast.136, f32[256]{0:T(256)S(1)} %bitcast.137, ...), kind=kLoop, calls=%fused_computation.196 | loop fusion | flops 51902464 | bytes 104916992 | tf_op jit(solution)/shard_map/reduce_sum | solution.py:50
  43.8 20.2 %psum.14 = f32[64,32]{1,0:T(8,128)S(1)} all-reduce(f32[64,32]{1,0:T(8,128)S(1)} %get-tuple-element.5), channel_id=1, replica_groups=mesh['row'=4,'col'=2,'blk'=4] {'blk'}, use_global_device_ids=true, to_apply=%region_1.0 | all-reduce | flops 2048 | bytes 16384 | tf_op jit(solution)/shard_map/psum | solution.py:50
  64.0 0.6 multiply_reduce_fusion
  64.6 24.0 %psum.15 = f32[64,32]{1,0:T(8,128)S(1)} all-reduce(f32[64,32]{1,0:T(8,128)S(1)} %multiply_reduce_fusion), channel_id=1, replica_groups=mesh['row'=4,'col'=2,'blk'=4] {'blk'}, use_global_device_ids=true, to_apply=%region_3.0 | all-reduce | flops 2048 | bytes 16384 | tf_op jit(solution)/shard_map/psum | solution.py:52
  88.6 1.5 add_convert_fusion.1
  90.1 8.6 %all-to-all-start = ((bf16[4,512,256]{2,1,0:T(8,128)(2,1)}), bf16[4,512,256]{2,1,0:T(8,128)(2,1)S(1)}, u32[]{:S(2)}, u32[]{:S(2)}) async-start(bf16[4,512,256]{2,1,0:T(8,128)(2,1)} %bitcast.132), calls=%async_computation | async-start | bytes 2097152 | tf_op jit(solution)/shard_map/all_to_all | solution.py:59
  98.8 60.8 %all_gather.10 = bf16[4096]{0:T(1024)(128)(2,1)S(1)} all-gather(bf16[1024]{0:T(1024)(128)(2,1)S(1)} %copy-done.3), channel_id=1, replica_groups=mesh['row'=4,'col'=2,'blk'=4] {'blk'}, dimensions={0}, use_global_device_ids=true | all-gather | bytes 10240 | tf_op jit(solution)/shard_map/all_gather | solution.py:62
  159.6 0.8 copy.15
  160.4 0.8 reshape.38
  161.2 24.6 %all-gather.3.cloned.1.call-done = bf16[4096,1024]{1,0:T(8,128)(2,1)} async-done(((bf16[1024,1024]{1,0:T(8,128)(2,1)}), bf16[4096,1024]{1,0:T(8,128)(2,1)}) %all-gather.3.cloned.1.call-update) | async-done | bytes 8388624 | tf_op jit(solution)/shard_map/all_gather | solution.py:60
  185.8 149.3 %all-gather.5.cloned.1.call-done = bf16[4096,1024]{1,0:T(8,128)(2,1)} async-done(((bf16[1024,1024]{1,0:T(8,128)(2,1)}), bf16[4096,1024]{1,0:T(8,128)(2,1)}) %all-gather.5.cloned.1.call-update) | async-done | bytes 8388624 | tf_op jit(solution)/shard_map/all_gather | solution.py:61
  335.1 28.7 %fusion.53 = bf16[4,512,1024]{2,1,0:T(8,128)(2,1)} fusion(bf16[4,1024,1024]{2,1,0:T(8,128)(2,1)} %bitcast.183, bf16[512,1024,1]{1,0,2:T(8,128)(2,1)S(1)} %reshape.38, bf16[4,1024,1024]{2,1,0:T(8,128)(2,1)} %bitcast.182, f32[4,1024]{1,0:T(4,128)S(1)} %reshape.36), kind=kOutput, calls=%fused_computation.57 | convolution fusion | flops 8730443776 | bytes 22036480 | tf_op jit(solution)/shard_map/kth,khc->ktc/dot_general | solution.py:31
  363.8 3.3 reduce_sum.32
  367.1 0.5 copy.16
  367.6 28.6 %all_to_all.32 = bf16[512,4,256]{0,2,1:T(8,128)(2,1)S(1)} all-to-all(bf16[512,4,256]{0,2,1:T(8,128)(2,1)S(1)} %bitcast.131), channel_id=1, replica_groups=mesh['row'=4,'col'=2,'blk'=4] {'blk'}, dimensions={1} | all-to-all | bytes 2097152 | tf_op jit(solution)/shard_map/all_to_all | solution.py:70
  396.3 0.3 convert_bitcast_fusion
  396.6 1.8 copy.17
  398.5 3.0 add_convert_fusion
  (27 shorter events, 0.2 us)
Async XLA Ops:
  6.5 1.5 copy-start
  6.5 5.8 %copy-start.2 = (f32[7,7,256]{2,1,0:T(8,128)S(1)}, f32[7,7,256]{2,1,0:T(8,128)}, u32[]{:S(2)}) copy-start(f32[7,7,256]{2,1,0:T(8,128)} %param.11) | copy-start | bytes 150532
  6.5 179.3 %all-gather.3.cloned.1.call-start = ((), (), s32[]{:S(2)}) async-start(), calls=%async_computation.2 | async-start | bytes 10485760 | tf_op jit(solution)/shard_map/all_gather | solution.py:60
  7.3 327.8 %all-gather.5.cloned.1.call-start = ((), (), s32[]{:S(2)}) async-start(), calls=%async_computation.3 | async-start | bytes 10485760 | tf_op jit(solution)/shard_map/all_gather | solution.py:61
  8.0 5.3 %collective-permute-start.1 = (bf16[3,32,256]{2,1,0:T(8,128)(2,1)S(1)}, bf16[3,32,256]{2,1,0:T(8,128)(2,1)S(1)}, u32[]{:S(2)}, u32[]{:S(2)}) collective-permute-start(bf16[3,32,256]{2,1,0:T(8,128)(2,1)S(1)} %get-tuple-element.9), channel_id=1, source_target_pairs={{8,0},{16,8},{24,16},{9,1},{17,9},{25,17},{10,2},{18,10},{26,18},{... | collective-permute-start | bytes 147464 | tf_op jit(solution)/shard_map/ppermute | solution.py:20
  9.3 3.9 collective-permute-start
  13.5 8.6 %collective-permute-start.2 = (bf16[70,3,256]{2,1,0:T(4,128)(2,1)S(1)}, bf16[70,3,256]{2,1,0:T(4,128)(2,1)S(1)}, u32[]{:S(2)}, u32[]{:S(2)}) collective-permute-start(bf16[70,3,256]{2,1,0:T(4,128)(2,1)S(1)} %get-tuple-element.7), channel_id=1, source_target_pairs={{0,4},{1,5},{2,6},{3,7},{8,12},{9,13},{10,14},{11,15},{16,20},{17,... | collective-permute-start | bytes 322568 | tf_op jit(solution)/shard_map/ppermute | solution.py:18
  18.3 8.3 %collective-permute-start.3 = (bf16[70,3,256]{2,1,0:T(4,128)(2,1)S(1)}, bf16[70,3,256]{2,1,0:T(4,128)(2,1)S(1)}, u32[]{:S(2)}, u32[]{:S(2)}) collective-permute-start(bf16[70,3,256]{2,1,0:T(4,128)(2,1)S(1)} %get-tuple-element.8), channel_id=1, source_target_pairs={{4,0},{5,1},{6,2},{7,3},{12,8},{13,9},{14,10},{15,11},{20,16},{21,... | collective-permute-start | bytes 322568 | tf_op jit(solution)/shard_map/ppermute | solution.py:20
  43.7 44.9 %copy-start.4 = (f32[256]{0:T(256)S(1)}, f32[256]{0:T(256)}, u32[]{:S(2)}) copy-start(f32[256]{0:T(256)} %param.14) | copy-start | bytes 3076
  43.8 44.9 %copy-start.5 = (f32[256]{0:T(256)S(1)}, f32[256]{0:T(256)}, u32[]{:S(2)}) copy-start(f32[256]{0:T(256)} %param.13) | copy-start | bytes 3076
  88.6 10.1 %copy-start.3 = (bf16[1024]{0:T(1024)(128)(2,1)S(1)}, bf16[1024]{0:T(1024)(128)(2,1)}, u32[]{:S(2)}) copy-start(bf16[1024]{0:T(1024)(128)(2,1)} %param.16) | copy-start | bytes 6148
  90.1 69.5 %all-to-all-start = ((bf16[4,512,256]{2,1,0:T(8,128)(2,1)}), bf16[4,512,256]{2,1,0:T(8,128)(2,1)S(1)}, u32[]{:S(2)}, u32[]{:S(2)}) async-start(bf16[4,512,256]{2,1,0:T(8,128)(2,1)} %bitcast.132), calls=%async_computation | async-start | bytes 2097152 | tf_op jit(solution)/shard_map/all_to_all | solution.py:59
  396.6 1.9 copy-start.1
  396.6 1.9 copy-start.6
  396.6 1.9 copy-start.7
Sparse Core Ops, SparseCore 0:
  8.9 176.8 all-gather.2
  187.4 147.6 all-gather.4
where the time goes:
time: 409 us; the launch traced here: 408 us
  waiting for transfers between devices  182 us (44%)
  blocking collectives  134 us (33%)
  matrix products  28.7 us (7%)
  other arithmetic  25.8 us (6%)
  starting transfers between devices  19.1 us (5%)
  between operations  13.6 us (3%)
  local copies, waits for them, and re-layouts  5.47 us (1%)
    all_gather x1, waiting for transfers between devices, shards(): w_second = lax.all_gather(w_out, 'blk', axis=0, tiled=True)  149 us
    all_gather x1, blocking collectives, shards(): b_first = lax.all_gather(b_in, 'blk', axis=0, tiled=True)  60.8 us
    dot_general x1, matrix products, shard_terms(): jnp.einsum('kth,khc->ktc', hidden, w_second, preferred_element_type=jnp.f...  28.7 us
    all_to_all x1, blocking collectives, shards(): lax.all_to_all(row_sums.astype(jnp.bfloat16), 'blk', split_axis=1, concat...  28.6 us
    all_gather x1, waiting for transfers between devices, shards(): w_first = lax.all_gather(w_in, 'blk', axis=0, tiled=True)  24.6 us
    psum x1, blocking collectives, shards(): spread = lax.psum(jnp.sum(centred * centred, axis=-1), 'blk') / C  24 us
    psum x1, blocking collectives, shards(): first_sum = lax.psum(jnp.sum(conv_out, axis=-1), 'blk')  20.2 us
    reduce_sum x1, other arithmetic, shards(): first_sum = lax.psum(jnp.sum(conv_out, axis=-1), 'blk')  16.4 us
  transfers between devices with their start and end apart: 7, of which 5 were waited for; matrix products, arithmetic and copies ran while one was open for 5% of the time, Pallas kernels for 0%

commit v1 on v0

v1 whole, which is shorter than its diff:
```python
import jax
import jax.numpy as jnp
from jax import lax
from jax.experimental import pallas as pl
from jax.experimental.pallas import tpu as pltpu
from jax.sharding import Mesh, PartitionSpec as P

KS = 7


def with_halo(cells, sides, width):
    for axis, dim in sides:
        count = lax.axis_size(axis)
        ends = count - 1
        head = lax.slice_in_dim(cells, 0, width, axis=dim)
        tail = lax.slice_in_dim(cells, cells.shape[dim] - width, cells.shape[dim], axis=dim)
        cells = jnp.concatenate(
            [
                lax.ppermute(tail, axis, [(i, (i + 1) % count) for i in range(ends)]),
                cells,
                lax.ppermute(head, axis, [((i + 1) % count, i) for i in range(ends)]),
            ],
            axis=dim,
        )
    return cells


def rotated(value, shift):
    count = lax.axis_size("blk")
    return lax.ppermute(value, "blk", [(i, (i + shift) % count) for i in range(count)])


def gathered(weights):
    half = weights.shape[0] // 2
    part = half // (lax.axis_size("y") * lax.axis_size("col"))
    place = lax.axis_index("y") * lax.axis_size("col") + lax.axis_index("col")
    own = lax.dynamic_slice_in_dim(
        weights, lax.axis_index("core") * half + place * part, part, axis=0
    )
    return lax.all_gather(own, ("blk", "y", "col"), axis=0, tiled=True)


def mlp_kernel(own_ref, peer_ref, first_ref, bias_ref, second_ref, own_out, peer_out, total):
    step = pl.program_id(0)

    @pl.when(step == 0)
    def _():
        own_out[...] = jnp.zeros_like(own_out)
        total[...] = jnp.zeros_like(total)

    bias = bias_ref[...].astype(jnp.float32)
    for rows, sums in ((peer_ref, total), (own_ref, own_out)):
        pre_act = lax.dot_general(
            rows[...], first_ref[...], (((1,), (1,)), ((), ())), preferred_element_type=jnp.float32
        )
        pre_act = pre_act + bias
        hidden = 0.5 * pre_act * (1.0 + lax.erf(pre_act * 0.7071067811865476))
        sums[...] += jnp.dot(
            hidden.astype(jnp.bfloat16), second_ref[...], preferred_element_type=jnp.float32
        )

    @pl.when(step == pl.num_programs(0) - 1)
    def _():
        peer_out[...] = total[...].astype(peer_out.dtype)


def mlp_terms(own, peer, w_first, bias, w_second):
    count, chans = own.shape
    hid = w_first.shape[0]
    tile = min(256, hid)
    whole = pl.BlockSpec((count, chans), lambda i: (0, 0))
    return pl.pallas_call(
        mlp_kernel,
        grid=(hid // tile,),
        in_specs=[
            whole,
            whole,
            pl.BlockSpec((tile, chans), lambda i: (i, 0)),
            pl.BlockSpec((1, tile), lambda i: (0, i)),
            pl.BlockSpec((tile, chans), lambda i: (i, 0)),
        ],
        out_specs=[whole, whole],
        out_shape=[
            jax.ShapeDtypeStruct((count, chans), jnp.float32),
            jax.ShapeDtypeStruct((count, chans), jnp.bfloat16),
        ],
        scratch_shapes=[pltpu.VMEM((count, chans), jnp.float32)],
        compiler_params=pltpu.CompilerParams(vmem_limit_bytes=32 * 1024 * 1024),
        cost_estimate=pl.CostEstimate(
            flops=8 * count * chans * hid, bytes_accessed=16 * count * chans, transcendentals=0
        ),
    )(own, peer, w_first, bias, w_second)


def shards(pixels, dw_kernel, dw_bias, ln_gain, ln_bias, w_in, b_in, w_out, b_out, layer_scale):
    tile_rows, tile_cols, chans = pixels.shape
    reach = (KS - 1) // 2
    blks = lax.axis_size("blk")
    w_first = gathered(w_in)
    w_second = gathered(w_out)
    b_first = lax.all_gather(
        lax.dynamic_slice_in_dim(
            b_in, lax.axis_index("core") * (b_in.shape[0] // 2), b_in.shape[0] // 2
        ),
        "blk",
        axis=0,
        tiled=True,
    )
    padded = with_halo(pixels, ((("y", "core"), 0), ("col", 1)), reach).astype(jnp.float32)
    conv_out = jnp.zeros((tile_rows, tile_cols, chans), jnp.float32) + dw_bias
    for row_off in range(KS):
        for col_off in range(KS):
            conv_out = (
                conv_out
                + padded[row_off : row_off + tile_rows, col_off : col_off + tile_cols, :]
                * dw_kernel[row_off, col_off]
            )
    part_mean = jnp.mean(conv_out, axis=-1)
    off = conv_out - part_mean[..., None]
    part_sq = jnp.sum(off * off, axis=-1)
    stats = jnp.stack([part_mean, part_sq])
    everyone = [stats] + [rotated(stats, k) for k in range(1, blks)]
    mean = sum(s[0] for s in everyone) / blks
    sq = sum(s[1] + chans * (s[0] - mean) ** 2 for s in everyone)
    spread = sq / (chans * blks)
    normed = (
        (conv_out - mean[..., None]) * lax.rsqrt(spread + 1e-06)[..., None] * ln_gain + ln_bias
    ).astype(jnp.bfloat16)
    pixel_count = tile_rows * tile_cols
    own_px = pixel_count // blks
    flat = normed.reshape(blks, own_px, chans)
    regrouped = lax.all_to_all(flat.reshape(pixel_count, chans), "blk", split_axis=0, concat_axis=1, tiled=True)
    swap = [(0, 1), (1, 0)]
    peer = lax.ppermute(regrouped, "core", swap)
    kept, sent = mlp_terms(regrouped, peer, w_first, b_first[None, :], w_second)
    mlp = kept + lax.ppermute(sent, "core", swap).astype(jnp.float32)
    mlp = mlp.astype(jnp.bfloat16)
    summed = lax.all_to_all(mlp, "blk", split_axis=1, concat_axis=0, tiled=True)
    result = pixels.astype(jnp.float32) + layer_scale * (
        summed.astype(jnp.float32).reshape(tile_rows, tile_cols, chans) + b_out
    )
    return result.astype(jnp.bfloat16)


def solution(mesh):
    row, col, blk = (mesh.shape[name] for name in ("row", "col", "blk"))
    split = Mesh(mesh.devices.reshape(row // 2, 2, col, blk), ("y", "core", "col", "blk"))
    placed = (
        P(("y", "core"), "col", "blk"),
        P(None, None, "blk"),
        P("blk"),
        P("blk"),
        P("blk"),
        P("blk", None),
        P("blk"),
        P("blk", None),
        P("blk"),
        P("blk"),
    )
    return jax.shard_map(
        shards, mesh=split, in_specs=placed, out_specs=P(("y", "core"), "col", "blk"), check_vma=False
    )
```

time: 409 us -> 258 us (0.63)
  waiting for transfers between devices: 182 us -> 80.8 us
  blocking collectives: 134 us -> 89.6 us
  matrix products: 28.7 us -> 0 us
  Pallas kernels: 0 us -> 20.3 us
  local copies, waits for them, and re-layouts: 5.47 us -> 14.9 us
    all_gather x2, waiting for transfers between devices: 174 us -> 66.4 us  [gathered(): return lax.all_gather(own, ('blk', 'y', 'col'), axis=0, tiled=True)]
    all_to_all x1 -> x2, blocking collectives: 28.6 us -> 77.8 us  [the longest x1 48.7 us: shards(): lax.all_to_all(flat.reshape(pixel_count, chans), 'blk', split_axis=0, con...]
    all_gather x1, blocking collectives: 60.8 us -> 11.9 us  [shards(): lax.all_gather(lax.dynamic_slice_in_dim(b_in, lax.axis_index('core') * (b...]
    psum x2 -> x0, blocking collectives: 44.2 us -> none  [the longest x1 24 us: shards(): spread = lax.psum(jnp.sum(centred * centred, axis=-1), 'blk') / C]
    dot_general x1 -> x0, matrix products: 28.7 us -> none  [shard_terms(): jnp.einsum('kth,khc->ktc', hidden, w_second, preferred_element_type=jnp.f...]
    pallas_call x0 -> x1, Pallas kernels: none -> 20.3 us  [mlp_terms(): pl.pallas_call(mlp_kernel, grid=(hid // tile,), in_specs=[whole, whole, p...]
    ppermute x0 -> x5, waiting for transfers between devices: none -> 8.78 us  [the longest x3 6.13 us: rotated(): lax.ppermute(value, 'blk', [(i, (i + shift) % count) for i in range(count)])]
    all_to_all x1 -> x0, starting transfers between devices: 8.63 us -> none  [shards(): lax.all_to_all(flat_rows, 'blk', split_axis=0, concat_axis=1, tiled=True)]
  transfers between devices with their start and end apart: 7 -> 11, of which waited for: 5 -> 6; matrix products, arithmetic and copies ran while one was open for 5% -> 11% of each run, Pallas kernels for 0% -> 0%
where the time goes in v1:
time: 258 us; the launch traced here: 257 us
  blocking collectives  89.6 us (35%)
  waiting for transfers between devices  80.8 us (31%)
  other arithmetic  22.9 us (9%)
  Pallas kernels  20.3 us (8%)
  starting transfers between devices  15.3 us (6%)
  local copies, waits for them, and re-layouts  14.9 us (6%)
  between operations  13.7 us (5%)
    all_gather x2, waiting for transfers between devices, gathered(): return lax.all_gather(own, ('blk', 'y', 'col'), axis=0, tiled=True)  66.4 us
    all_to_all x1, blocking collectives, shards(): lax.all_to_all(flat.reshape(pixel_count, chans), 'blk', split_axis=0, con...  48.7 us
    all_to_all x1, blocking collectives, shards(): summed = lax.all_to_all(mlp, 'blk', split_axis=1, concat_axis=0, tiled=True)  29 us
    pallas_call x1, Pallas kernels, mlp_terms(): pl.pallas_call(mlp_kernel, grid=(hid // tile,), in_specs=[whole, whole, p...  20.3 us
    reduce_sum x1, other arithmetic, shards(): part_mean = jnp.mean(conv_out, axis=-1)  17.2 us
    all_gather x1, blocking collectives, shards(): lax.all_gather(lax.dynamic_slice_in_dim(b_in, lax.axis_index('core') * (b...  11.9 us
    ppermute x2, starting transfers between devices, with_halo(): lax.ppermute(tail, axis, [(i, (i + 1) % count) for i in range(ends)])  7.88 us
    unnamed x25, local copies, waits for them, and re-layouts  7.12 us
  transfers between devices with their start and end apart: 11, of which 6 were waited for; matrix products, arithmetic and copies ran while one was open for 11% of the time, Pallas kernels for 0%

profile of v1, /device:TPU:0, one launch (start us, length us, event | category | flops | bytes accessed | tf_op | source)
XLA Modules:
  0.0 257.5 jit_solution(5553709215163718301)
XLA Ops:
  6.5 1.6 copy-done
  8.1 0.7 constant_dynamic-slice_fusion.1
  8.9 0.8 fusion.62
  9.8 1.3 collective-permute-start.1
  11.0 3.0 %collective-permute-start = (bf16[3,32,256]{2,1,0:T(8,128)(2,1)S(1)}, bf16[3,32,256]{2,1,0:T(8,128)(2,1)S(1)}, u32[]{:S(2)}, u32[]{:S(2)}) collective-permute-start(bf16[3,32,256]{2,1,0:T(8,128)(2,1)S(1)} %get-tuple-element.16), channel_id=1, source_target_pairs={{0,8},{8,16},{16,24},{1,9},{9,17},{17,25},{2,10},{10,18},{18,26},{... | collective-permute-start | bytes 147464 | tf_op jit(solution)/shard_map/ppermute | solution.py:19
  14.1 1.7 constant_dynamic-slice_fusion
  15.8 1.0 fusion.63
  16.8 1.6 fusion.64
  18.7 4.9 %collective-permute-start.2 = (bf16[70,3,256]{2,1,0:T(4,128)(2,1)S(1)}, bf16[70,3,256]{2,1,0:T(4,128)(2,1)S(1)}, u32[]{:S(2)}, u32[]{:S(2)}) collective-permute-start(bf16[70,3,256]{2,1,0:T(4,128)(2,1)S(1)} %get-tuple-element.13), channel_id=1, source_target_pairs={{0,4},{1,5},{2,6},{3,7},{8,12},{9,13},{10,14},{11,15},{16,20},{17,... | collective-permute-start | bytes 322568 | tf_op jit(solution)/shard_map/ppermute | solution.py:19
  23.5 1.3 collective-permute-start.3
  24.8 1.5 fusion.65
  26.4 1.1 collective-permute-done.2
  27.5 4.5 %collective-permute-done.3 = bf16[70,3,256]{2,1,0:T(4,128)(2,1)S(1)} collective-permute-done((bf16[70,3,256]{2,1,0:T(4,128)(2,1)S(1)}, bf16[70,3,256]{2,1,0:T(4,128)(2,1)S(1)}, u32[]{:S(2)}, u32[]{:S(2)}) %collective-permute-start.3) | collective-permute-done | bytes 107552 | tf_op jit(solution)/shard_map/ppermute | solution.py:21
  31.9 0.6 maximum_convert_fusion
  32.6 17.2 %fusion.59 = (f32[64,32]{1,0:T(8,128)S(1)}, f32[64,32,256]{2,1,0:T(8,128)}) fusion(f32[256]{0:T(256)} %bitcast.169, f32[70,38,256]{2,1,0:T(8,128)S(1)} %maximum_convert_fusion, f32[256]{0:T(256)} %bitcast.170, f32[256]{0:T(256)S(1)} %bitcast.123, f32[256]{0:T(256)S(1)} %bitcast.124, f32[256]{0:T(256)S(1)} %bitcast.125, f32[256]{0:T(256)S(1)} %bitcast.126, ...), kind=kLoop, calls=%fused_computation.128 | loop fusion | flops 51902464 | bytes 104916992 | tf_op jit(solution)/shard_map/reduce_sum | solution.py:118
  49.8 2.4 multiply_reduce_fusion
  52.2 3.6 %collective-permute-start.6 = (f32[2,64,32]{2,1,0:T(8,128)S(1)}, f32[2,64,32]{2,1,0:T(8,128)S(1)}, u32[]{:S(2)}, u32[]{:S(2)}) collective-permute-start(f32[2,64,32]{2,1,0:T(8,128)S(1)} %pad_maximum_fusion), channel_id=1, source_target_pairs={{0,3},{1,0},{2,1},{3,2},{4,7},{5,4},{6,5},{7,6},{8,11},{9,8},{10,9... | collective-permute-start | bytes 49160 | tf_op jit(solution)/shard_map/ppermute | solution.py:30
  55.8 1.0 collective-permute-start.4
  56.8 1.5 collective-permute-done.6
  58.3 4.7 %collective-permute-done.5 = f32[2,64,32]{2,1,0:T(8,128)S(1)} collective-permute-done((f32[2,64,32]{2,1,0:T(8,128)S(1)}, f32[2,64,32]{2,1,0:T(8,128)S(1)}, u32[]{:S(2)}, u32[]{:S(2)}) %collective-permute-start.5) | collective-permute-done | bytes 16416 | tf_op jit(solution)/shard_map/ppermute | solution.py:30
  63.1 0.7 add_convert_fusion.2
  63.8 48.7 %all_to_all.32 = bf16[4,512,256]{2,1,0:T(8,128)(2,1)S(1)} all-to-all(bf16[4,512,256]{2,1,0:T(8,128)(2,1)S(1)} %bitcast.119), channel_id=1, replica_groups=mesh['y'=2,'core'=2,'col'=2,'blk'=4] {'blk'}, dimensions={0} | all-to-all | bytes 2097152 | tf_op jit(solution)/shard_map/all_to_all | solution.py:132
  112.9 11.9 %all-gather = bf16[4,1,512]{2,1,0:T(2,128)(2,1)S(1)} all-gather(bf16[1,1,512]{2,1,0:T(2,128)(2,1)S(1)} %reshape.103), channel_id=1, replica_groups=mesh['y'=2,'core'=2,'col'=2,'blk'=4] {'blk'}, dimensions={0}, use_global_device_ids=true | all-gather | bytes 5120 | tf_op jit(solution)/shard_map/all_gather | solution.py:101
  124.7 66.4 %all-gather.6.cloned.1.call-done.second_ref = bf16[2048,1024]{1,0:T(8,128)(2,1)} async-done(((bf16[128,1024]{1,0:T(8,128)(2,1)}), bf16[2048,1024]{1,0:T(8,128)(2,1)}) %all-gather.6.cloned.1.call-update) | async-done | bytes 4194320 | tf_op jit(solution)/shard_map/all_gather | solution.py:40
  191.1 2.2 copy-done.1
  193.3 2.2 copy-done.2
  195.5 20.3 %shard_map.100 = (f32[512,1024]{1,0:T(8,128)S(1)}, bf16[512,1024]{1,0:T(8,128)(2,1)S(1)}) custom-call(bf16[512,1024]{1,0:T(8,128)(2,1)S(1)} %bitcast.114, bf16[512,1024]{1,0:T(8,128)(2,1)} %collective-permute-done.7.peer_ref, bf16[2048,1024]{1,0:T(8,128)(2,1)S(1)} %copy-done.1, bf16[1,2048]{1,0:T(2,128)(2,1)S(1)} %bitcast.115, bf16[2048,1024]{1,0:T(8,128)(2,1)S(1)} %copy-done.2), custom_call_target="tpu_custom_call" | custom-call | flops 8589934592 | bytes 8388608 | tf_op jit(solution)/shard_map/pallas_call | solution.py:72
  215.9 2.6 %collective-permute-done.8 = bf16[512,1024]{1,0:T(8,128)(2,1)S(1)} collective-permute-done((bf16[512,1024]{1,0:T(8,128)(2,1)S(1)}, bf16[512,1024]{1,0:T(8,128)(2,1)S(1)}, u32[]{:S(2)}, u32[]{:S(2)}) %collective-permute-start.8) | collective-permute-done | bytes 1048608 | tf_op jit(solution)/shard_map/ppermute | solution.py:136
  218.5 0.4 add_convert_fusion.1
  219.0 29.0 %all_to_all.33 = bf16[512,4,256]{2,0,1:T(8,128)(2,1)S(1)} all-to-all(bf16[512,4,256]{2,0,1:T(8,128)(2,1)S(1)} %bitcast.118), channel_id=1, replica_groups=mesh['y'=2,'core'=2,'col'=2,'blk'=4] {'blk'}, dimensions={1} | all-to-all | bytes 2097152 | tf_op jit(solution)/shard_map/all_to_all | solution.py:138
  248.2 1.0 copy-done.5
  249.2 1.4 add_convert_fusion
  (42 shorter events, 1.0 us)
Async XLA Ops:
  6.5 1.6 copy-start
  6.5 11.9 %copy-start.4 = (bf16[64,32,256]{2,1,0:T(8,128)(2,1)S(1)}, bf16[64,32,256]{2,1,0:T(8,128)(2,1)}, u32[]{:S(2)}) copy-start(bf16[64,32,256]{2,1,0:T(8,128)(2,1)} %param.10) | copy-start | bytes 3145732
  6.5 118.2 %all-gather.4.cloned.1.call-start = ((), (), s32[]{:S(2)}) async-start(), calls=%async_computation.2 | async-start | bytes 4456448 | tf_op jit(solution)/shard_map/all_gather | solution.py:40
  8.9 182.2 %all-gather.6.cloned.1.call-start = ((), (), s32[]{:S(2)}) async-start(), calls=%async_computation.3 | async-start | bytes 4456448 | tf_op jit(solution)/shard_map/all_gather | solution.py:40
  9.8 8.8 %collective-permute-start.1 = (bf16[3,32,256]{2,1,0:T(8,128)(2,1)S(1)}, bf16[3,32,256]{2,1,0:T(8,128)(2,1)S(1)}, u32[]{:S(2)}, u32[]{:S(2)}) collective-permute-start(bf16[3,32,256]{2,1,0:T(8,128)(2,1)S(1)} %get-tuple-element.15), channel_id=1, source_target_pairs={{8,0},{16,8},{24,16},{9,1},{17,9},{25,17},{10,2},{18,10},{26,18},{... | collective-permute-start | bytes 147464 | tf_op jit(solution)/shard_map/ppermute | solution.py:21
  11.0 7.4 %collective-permute-start = (bf16[3,32,256]{2,1,0:T(8,128)(2,1)S(1)}, bf16[3,32,256]{2,1,0:T(8,128)(2,1)S(1)}, u32[]{:S(2)}, u32[]{:S(2)}) collective-permute-start(bf16[3,32,256]{2,1,0:T(8,128)(2,1)S(1)} %get-tuple-element.16), channel_id=1, source_target_pairs={{0,8},{8,16},{16,24},{1,9},{9,17},{17,25},{2,10},{10,18},{18,26},{... | collective-permute-start | bytes 147464 | tf_op jit(solution)/shard_map/ppermute | solution.py:19
  18.7 8.8 %collective-permute-start.2 = (bf16[70,3,256]{2,1,0:T(4,128)(2,1)S(1)}, bf16[70,3,256]{2,1,0:T(4,128)(2,1)S(1)}, u32[]{:S(2)}, u32[]{:S(2)}) collective-permute-start(bf16[70,3,256]{2,1,0:T(4,128)(2,1)S(1)} %get-tuple-element.13), channel_id=1, source_target_pairs={{0,4},{1,5},{2,6},{3,7},{8,12},{9,13},{10,14},{11,15},{16,20},{17,... | collective-permute-start | bytes 322568 | tf_op jit(solution)/shard_map/ppermute | solution.py:19
  23.5 8.4 %collective-permute-start.3 = (bf16[70,3,256]{2,1,0:T(4,128)(2,1)S(1)}, bf16[70,3,256]{2,1,0:T(4,128)(2,1)S(1)}, u32[]{:S(2)}, u32[]{:S(2)}) collective-permute-start(bf16[70,3,256]{2,1,0:T(4,128)(2,1)S(1)} %get-tuple-element.14), channel_id=1, source_target_pairs={{4,0},{5,1},{6,2},{7,3},{12,8},{13,9},{14,10},{15,11},{20,16},{21,... | collective-permute-start | bytes 322568 | tf_op jit(solution)/shard_map/ppermute | solution.py:21
  49.7 13.3 %copy-start.3 = (f32[64,32,256]{2,1,0:T(8,128)S(1)}, f32[64,32,256]{2,1,0:T(8,128)}, u32[]{:S(2)}) copy-start(f32[64,32,256]{2,1,0:T(8,128)} %get-tuple-element.12) | copy-start | bytes 6291460
  49.7 13.3 %copy-start.6 = (f32[256]{0:T(256)S(1)}, f32[256]{0:T(256)}, u32[]{:S(2)}) copy-start(f32[256]{0:T(256)} %param.14) | copy-start | bytes 3076
  49.7 13.3 %copy-start.7 = (f32[256]{0:T(256)S(1)}, f32[256]{0:T(256)}, u32[]{:S(2)}) copy-start(f32[256]{0:T(256)} %param.13) | copy-start | bytes 3076
  52.2 6.1 %collective-permute-start.6 = (f32[2,64,32]{2,1,0:T(8,128)S(1)}, f32[2,64,32]{2,1,0:T(8,128)S(1)}, u32[]{:S(2)}, u32[]{:S(2)}) collective-permute-start(f32[2,64,32]{2,1,0:T(8,128)S(1)} %pad_maximum_fusion), channel_id=1, source_target_pairs={{0,3},{1,0},{2,1},{3,2},{4,7},{5,4},{6,5},{7,6},{8,11},{9,8},{10,9... | collective-permute-start | bytes 49160 | tf_op jit(solution)/shard_map/ppermute | solution.py:30
  55.8 7.2 %collective-permute-start.5 = (f32[2,64,32]{2,1,0:T(8,128)S(1)}, f32[2,64,32]{2,1,0:T(8,128)S(1)}, u32[]{:S(2)}, u32[]{:S(2)}) collective-permute-start(f32[2,64,32]{2,1,0:T(8,128)S(1)} %pad_maximum_fusion), channel_id=1, source_target_pairs={{0,2},{1,3},{2,0},{3,1},{4,6},{5,7},{6,4},{7,5},{8,10},{9,11},{10,... | collective-permute-start | bytes 49160 | tf_op jit(solution)/shard_map/ppermute | solution.py:30
  55.8 7.2 %collective-permute-start.4 = (f32[2,64,32]{2,1,0:T(8,128)S(1)}, f32[2,64,32]{2,1,0:T(8,128)S(1)}, u32[]{:S(2)}, u32[]{:S(2)}) collective-permute-start(f32[2,64,32]{2,1,0:T(8,128)S(1)} %pad_maximum_fusion), channel_id=1, source_target_pairs={{0,1},{1,2},{2,3},{3,0},{4,5},{5,6},{6,7},{7,4},{8,9},{9,10},{10,1... | collective-permute-start | bytes 49160 | tf_op jit(solution)/shard_map/ppermute | solution.py:30
  63.8 49.0 %copy-start.10 = (bf16[1024]{0:T(1024)(128)(2,1)S(1)}, bf16[1024]{0:T(1024)(128)(2,1)}, u32[]{:S(2)}) copy-start(bf16[1024]{0:T(1024)(128)(2,1)} %param.16) | copy-start | bytes 6148
  112.7 12.0 %collective-permute-start.7 = (bf16[512,1024]{1,0:T(8,128)(2,1)S(1)}, bf16[512,1024]{1,0:T(8,128)(2,1)}, u32[]{:S(2)}, u32[]{:S(2)}) collective-permute-start(bf16[512,1024]{1,0:T(8,128)(2,1)S(1)} %bitcast.113), channel_id=1, source_target_pairs={{0,8},{8,0},{1,9},{9,1},{2,10},{10,2},{3,11},{11,3},{4,12},{12,4},... | collective-permute-start | bytes 3145736 | tf_op jit(solution)/shard_map/ppermute | solution.py:134
  191.1 2.2 copy-start.1
  193.3 2.2 copy-start.2
  215.8 2.7 %collective-permute-start.8 = (bf16[512,1024]{1,0:T(8,128)(2,1)S(1)}, bf16[512,1024]{1,0:T(8,128)(2,1)S(1)}, u32[]{:S(2)}, u32[]{:S(2)}) collective-permute-start(bf16[512,1024]{1,0:T(8,128)(2,1)S(1)} %get-tuple-element.8), channel_id=1, source_target_pairs={{0,8},{8,0},{1,9},{9,1},{2,10},{10,2},{3,11},{11,3},{4,12},{12,4},... | collective-permute-start | bytes 3145736 | tf_op jit(solution)/shard_map/ppermute | solution.py:136
  248.0 1.2 copy-start.5
  248.0 1.2 copy-start.8
  248.0 1.2 copy-start.9
Sparse Core Ops, SparseCore 0:
  10.1 101.6 all-gather.3
  114.6 76.4 all-gather.5

commit v2 on v1

--- a/solution.py
+++ b/solution.py
@@ -38,6 +38,49 @@
         weights, lax.axis_index("core") * half + place * part, part, axis=0
     )
     return lax.all_gather(own, ("blk", "y", "col"), axis=0, tiled=True)
+
+
+def passed(w_in, b_in, w_out):
+    chans = w_in.shape[1]
+    half = w_in.shape[0] // 2
+    plane = lax.axis_size("y") * lax.axis_size("col")
+    part = half // plane
+    start = lax.axis_index("core") * half
+    place = lax.axis_index("y") * lax.axis_size("col") + lax.axis_index("col")
+    begin = start + place * part
+    bias_row = jnp.pad(
+        lax.dynamic_slice_in_dim(b_in, begin, part)[None, :], ((0, 15), (0, chans - part))
+    )
+    own = jnp.concatenate(
+        [
+            lax.dynamic_slice_in_dim(w_in, begin, part, axis=0),
+            lax.dynamic_slice_in_dim(w_out, begin, part, axis=0),
+            bias_row,
+        ]
+    )
+    pieces = []
+    for k in range(1, lax.axis_size("blk")):
+        arrived = rotated(own, k)
+        pieces.append(arrived)
+        for j in range(1, plane):
+            pieces.append(lax.ppermute(arrived, ("y", "col"), [(i, i ^ j) for i in range(plane)]))
+    w_first = [lax.dynamic_slice_in_dim(w_in, start, half, axis=0)] + [p[:part] for p in pieces]
+    w_second = [lax.dynamic_slice_in_dim(w_out, start, half, axis=0)] + [
+        p[part : 2 * part] for p in pieces
+    ]
+    bias = [lax.dynamic_slice_in_dim(b_in, start, half)] + [p[2 * part, :part] for p in pieces]
+    return jnp.concatenate(w_first), jnp.concatenate(bias), jnp.concatenate(w_second)
+
+
+def collected(w_in, b_in, w_out):
+    half = b_in.shape[0] // 2
+    b_first = lax.all_gather(
+        lax.dynamic_slice_in_dim(b_in, lax.axis_index("core") * half, half),
+        "blk",
+        axis=0,
+        tiled=True,
+    )
+    return gathered(w_in), b_first, gathered(w_out)
 
 
 def mlp_kernel(own_ref, peer_ref, first_ref, bias_ref, second_ref, own_out, peer_out, total):
@@ -96,16 +139,9 @@
     tile_rows, tile_cols, chans = pixels.shape
     reach = (KS - 1) // 2
     blks = lax.axis_size("blk")
-    w_first = gathered(w_in)
-    w_second = gathered(w_out)
-    b_first = lax.all_gather(
-        lax.dynamic_slice_in_dim(
-            b_in, lax.axis_index("core") * (b_in.shape[0] // 2), b_in.shape[0] // 2
-        ),
-        "blk",
-        axis=0,
-        tiled=True,
-    )
+    plane = lax.axis_size("y") * lax.axis_size("col")
+    few = plane in (1, 2, 4) and blks * plane <= 32
+    w_first, b_first, w_second = (passed if few else collected)(w_in, b_in, w_out)
     padded = with_halo(pixels, ((("y", "core"), 0), ("col", 1)), reach).astype(jnp.float32)
     conv_out = jnp.zeros((tile_rows, tile_cols, chans), jnp.float32) + dw_bias
     for row_off in range(KS):

time: 258 us -> 204 us (0.79)
  blocking collectives: 89.6 us -> 30.7 us
  starting transfers between devices: 15.3 us -> 57.8 us
  waiting for transfers between devices: 80.8 us -> 42.2 us
  local copies, waits for them, and re-layouts: 14.9 us -> 31.1 us
  between operations: 13.7 us -> 0.27 us
    all_gather x2 -> x0, waiting for transfers between devices: 66.4 us -> none  [gathered(): return lax.all_gather(own, ('blk', 'y', 'col'), axis=0, tiled=True)]
    all_to_all x1 -> x0, blocking collectives: 48.7 us -> none  [shards(): lax.all_to_all(flat.reshape(pixel_count, chans), 'blk', split_axis=0, con...]
    ppermute x0 -> x9, starting transfers between devices: none -> 35 us  [passed(): lax.ppermute(arrived, ('y', 'col'), [(i, i ^ j) for i in range(plane)])]
    ppermute x0 -> x9, waiting for transfers between devices: none -> 31.3 us  [passed(): lax.ppermute(arrived, ('y', 'col'), [(i, i ^ j) for i in range(plane)])]
    unnamed x25 -> x48, local copies, waits for them, and re-layouts: 7.12 us -> 22.9 us
    all_gather x1 -> x0, blocking collectives: 11.9 us -> none  [shards(): lax.all_gather(lax.dynamic_slice_in_dim(b_in, lax.axis_index('core') * (b...]
    ppermute x3 -> x6, starting transfers between devices: 4.66 us -> 10.3 us  [rotated(): lax.ppermute(value, 'blk', [(i, (i + shift) % count) for i in range(count)])]
    ppermute x3 -> x6, waiting for transfers between devices: 6.13 us -> 0.67 us  [rotated(): lax.ppermute(value, 'blk', [(i, (i + shift) % count) for i in range(count)])]
  transfers between devices with their start and end apart: 11 -> 22, of which waited for: 6 -> 10; matrix products, arithmetic and copies ran while one was open for 11% -> 21% of each run, Pallas kernels for 0% -> 0%
where the time goes in v2:
time: 204 us; the launch traced here: 203 us
  starting transfers between devices  57.8 us (28%)
  waiting for transfers between devices  42.2 us (21%)
  local copies, waits for them, and re-layouts  31.1 us (15%)
  blocking collectives  30.7 us (15%)
  other arithmetic  22.1 us (11%)
  Pallas kernels  19.1 us (9%)
    ppermute x9, starting transfers between devices, passed(): lax.ppermute(arrived, ('y', 'col'), [(i, i ^ j) for i in range(plane)])  35 us
    ppermute x9, waiting for transfers between devices, passed(): lax.ppermute(arrived, ('y', 'col'), [(i, i ^ j) for i in range(plane)])  31.3 us
    all_to_all x1, blocking collectives, shards(): summed = lax.all_to_all(mlp, 'blk', split_axis=1, concat_axis=0, tiled=True)  30.7 us
    unnamed x48, local copies, waits for them, and re-layouts  22.9 us
    pallas_call x1, Pallas kernels, mlp_terms(): pl.pallas_call(mlp_kernel, grid=(hid // tile,), in_specs=[whole, whole, p...  19.1 us
    reduce_sum x1, other arithmetic, shards(): part_mean = jnp.mean(conv_out, axis=-1)  16.5 us
    ppermute x6, starting transfers between devices, rotated(): lax.ppermute(value, 'blk', [(i, (i + shift) % count) for i in range(count)])  10.3 us
    ppermute x2, waiting for transfers between devices, with_halo(): lax.ppermute(head, axis, [((i + 1) % count, i) for i in range(ends)])  7.24 us
  transfers between devices with their start and end apart: 22, of which 10 were waited for; matrix products, arithmetic and copies ran while one was open for 21% of the time, Pallas kernels for 0%

profile of v2, /device:TPU:0, one launch (start us, length us, event | category | flops | bytes accessed | tf_op | source)
XLA Modules:
  0.0 203.2 jit_solution(14460620249824951414)
XLA Ops:
  2.8 3.0 %collective-permute-start.8 = (bf16[272,1024]{1,0:T(8,128)(2,1)}, bf16[272,1024]{1,0:T(8,128)(2,1)}, u32[]{:S(2)}, u32[]{:S(2)}) collective-permute-start(bf16[272,1024]{1,0:T(8,128)(2,1)} %fusion.50), channel_id=1, source_target_pairs={{0,1},{1,2},{2,3},{3,0},{4,5},{5,6},{6,7},{7,4},{8,9},{9,10},{10,1... | collective-permute-start | bytes 1671176 | tf_op jit(solution)/shard_map/ppermute | solution.py:30
  5.8 2.6 %collective-permute-start.12 = (bf16[272,1024]{1,0:T(8,128)(2,1)}, bf16[272,1024]{1,0:T(8,128)(2,1)}, u32[]{:S(2)}, u32[]{:S(2)}) collective-permute-start(bf16[272,1024]{1,0:T(8,128)(2,1)} %fusion.50), channel_id=1, source_target_pairs={{0,2},{1,3},{2,0},{3,1},{4,6},{5,7},{6,4},{7,5},{8,10},{9,11},{10,... | collective-permute-start | bytes 1671176 | tf_op jit(solution)/shard_map/ppermute | solution.py:30
  8.4 1.3 collective-permute-start
  11.7 2.9 %collective-permute-done.1 = bf16[3,32,256]{2,1,0:T(8,128)(2,1)S(1)} collective-permute-done((bf16[3,32,256]{2,1,0:T(8,128)(2,1)S(1)}, bf16[3,32,256]{2,1,0:T(8,128)(2,1)S(1)}, u32[]{:S(2)}, u32[]{:S(2)}) %collective-permute-start.1) | collective-permute-done | bytes 49184 | tf_op jit(solution)/shard_map/ppermute | solution.py:21
  14.7 3.4 %collective-permute-start.2 = (bf16[70,3,256]{2,1,0:T(4,128)(2,1)S(1)}, bf16[70,3,256]{2,1,0:T(4,128)(2,1)S(1)}, u32[]{:S(2)}, u32[]{:S(2)}) collective-permute-start(bf16[70,3,256]{2,1,0:T(4,128)(2,1)S(1)} %get-tuple-element.13), channel_id=1, source_target_pairs={{0,4},{1,5},{2,6},{3,7},{8,12},{9,13},{10,14},{11,15},{16,20},{17,... | collective-permute-start | bytes 322568 | tf_op jit(solution)/shard_map/ppermute | solution.py:19
  20.7 4.4 %collective-permute-done.3 = bf16[70,3,256]{2,1,0:T(4,128)(2,1)S(1)} collective-permute-done((bf16[70,3,256]{2,1,0:T(4,128)(2,1)S(1)}, bf16[70,3,256]{2,1,0:T(4,128)(2,1)S(1)}, u32[]{:S(2)}, u32[]{:S(2)}) %collective-permute-start.3) | collective-permute-done | bytes 107552 | tf_op jit(solution)/shard_map/ppermute | solution.py:21
  25.7 16.5 %fusion.61 = (f32[64,32]{1,0:T(8,128)S(1)}, f32[64,32,256]{2,1,0:T(8,128)S(1)}) fusion(f32[256]{0:T(256)} %bitcast.192, f32[70,38,256]{2,1,0:T(8,128)S(1)} %maximum_convert_fusion, f32[256]{0:T(256)} %bitcast.193, f32[256]{0:T(256)S(1)} %bitcast.146, f32[256]{0:T(256)S(1)} %bitcast.147, f32[256]{0:T(256)S(1)} %bitcast.148, f32[256]{0:T(256)S(1)} %bitcast.149, ...), kind=kLoop, calls=%fused_computation.170 | loop fusion | flops 51902464 | bytes 104916992 | tf_op jit(solution)/shard_map/reduce_sum | solution.py:154
  43.2 1.7 collective-permute-start.5
  44.9 1.9 collective-permute-start.6
  46.9 2.7 %dynamic-slice_dynamic-update-slice_fusion = (bf16[2048,1024]{1,0:T(8,128)(2,1)}, bf16[2048,1024]{1,0:T(8,128)(2,1)}) fusion(bf16[1024,1024]{1,0:T(8,128)(2,1)S(1)} %copy-done.4, s32[]{:T(128)S(6)} %select_n.4, bf16[1024,1024]{1,0:T(8,128)(2,1)} %param.15), kind=kLoop, calls=%fused_computation.106 | loop fusion | bytes 4194308
  51.4 1.5 add_convert_fusion.2
  52.9 4.6 %all-to-all-start = ((bf16[4,512,256]{2,1,0:T(8,128)(2,1)}), bf16[4,512,256]{2,1,0:T(8,128)(2,1)S(1)}, u32[]{:S(2)}, u32[]{:S(2)}) async-start(bf16[4,512,256]{2,1,0:T(8,128)(2,1)} %bitcast.57), calls=%async_computation | async-start | bytes 2097152 | tf_op jit(solution)/shard_map/all_to_all | solution.py:168
  58.4 10.3 %collective-permute-start.10 = (bf16[272,1024]{1,0:T(8,128)(2,1)}, bf16[272,1024]{1,0:T(8,128)(2,1)S(1)}, u32[]{:S(2)}, u32[]{:S(2)}) collective-permute-start(bf16[272,1024]{1,0:T(8,128)(2,1)} %collective-permute-done.8), channel_id=1, source_target_pairs={{0,16},{4,20},{16,0},{20,4},{1,17},{5,21},{17,1},{21,5},{2,18},{6,... | collective-permute-start | bytes 1671176 | tf_op jit(solution)/shard_map/ppermute | solution.py:66
  68.7 1.4 collective-permute-start.11
  71.4 1.9 slice_dynamic-update-slice_fusion.11
  73.2 1.5 collective-permute-start.14
  75.4 8.4 %collective-permute-start.15 = (bf16[272,1024]{1,0:T(8,128)(2,1)}, bf16[272,1024]{1,0:T(8,128)(2,1)S(1)}, u32[]{:S(2)}, u32[]{:S(2)}) collective-permute-start(bf16[272,1024]{1,0:T(8,128)(2,1)} %collective-permute-done.12), channel_id=1, source_target_pairs={{0,20},{4,16},{16,4},{20,0},{1,21},{5,17},{17,5},{21,1},{2,22},{6,... | collective-permute-start | bytes 1671176 | tf_op jit(solution)/shard_map/ppermute | solution.py:66
  84.7 9.4 %collective-permute-done.10 = bf16[272,1024]{1,0:T(8,128)(2,1)S(1)} collective-permute-done((bf16[272,1024]{1,0:T(8,128)(2,1)}, bf16[272,1024]{1,0:T(8,128)(2,1)S(1)}, u32[]{:S(2)}, u32[]{:S(2)}) %collective-permute-start.10) | collective-permute-done | bytes 557088 | tf_op jit(solution)/shard_map/ppermute | solution.py:66
  94.0 2.3 %collective-permute-start.17 = (bf16[272,1024]{1,0:T(8,128)(2,1)}, bf16[272,1024]{1,0:T(8,128)(2,1)S(1)}, u32[]{:S(2)}, u32[]{:S(2)}) collective-permute-start(bf16[272,1024]{1,0:T(8,128)(2,1)} %collective-permute-done.16), channel_id=1, source_target_pairs={{0,4},{4,0},{16,20},{20,16},{1,5},{5,1},{17,21},{21,17},{2,6},{6,2... | collective-permute-start | bytes 1671176 | tf_op jit(solution)/shard_map/ppermute | solution.py:66
  97.9 9.8 %collective-permute-start.19 = (bf16[272,1024]{1,0:T(8,128)(2,1)}, bf16[272,1024]{1,0:T(8,128)(2,1)}, u32[]{:S(2)}, u32[]{:S(2)}) collective-permute-start(bf16[272,1024]{1,0:T(8,128)(2,1)} %collective-permute-done.16), channel_id=1, source_target_pairs={{0,20},{4,16},{16,4},{20,0},{1,21},{5,17},{17,5},{21,1},{2,22},{6,... | collective-permute-start | bytes 1671176 | tf_op jit(solution)/shard_map/ppermute | solution.py:66
  107.7 10.5 %collective-permute-done.14 = bf16[272,1024]{1,0:T(8,128)(2,1)S(1)} collective-permute-done((bf16[272,1024]{1,0:T(8,128)(2,1)}, bf16[272,1024]{1,0:T(8,128)(2,1)S(1)}, u32[]{:S(2)}, u32[]{:S(2)}) %collective-permute-start.14) | collective-permute-done | bytes 557088 | tf_op jit(solution)/shard_map/ppermute | solution.py:66
  119.1 2.8 %collective-permute-done.17 = bf16[272,1024]{1,0:T(8,128)(2,1)S(1)} collective-permute-done((bf16[272,1024]{1,0:T(8,128)(2,1)}, bf16[272,1024]{1,0:T(8,128)(2,1)S(1)}, u32[]{:S(2)}, u32[]{:S(2)}) %collective-permute-start.17) | collective-permute-done | bytes 557088 | tf_op jit(solution)/shard_map/ppermute | solution.py:66
  121.9 1.9 slice_dynamic-update-slice_fusion.7
  124.5 8.5 %collective-permute-done.18 = bf16[272,1024]{1,0:T(8,128)(2,1)S(1)} collective-permute-done((bf16[272,1024]{1,0:T(8,128)(2,1)}, bf16[272,1024]{1,0:T(8,128)(2,1)S(1)}, u32[]{:S(2)}, u32[]{:S(2)}) %collective-permute-start.18) | collective-permute-done | bytes 557088 | tf_op jit(solution)/shard_map/ppermute | solution.py:66
  137.7 1.9 slice_dynamic-update-slice_fusion.3
  141.3 1.9 slice_dynamic-update-slice_fusion
  143.2 2.2 %copy-done = bf16[2048,1024]{1,0:T(8,128)(2,1)S(1)} copy-done((bf16[2048,1024]{1,0:T(8,128)(2,1)S(1)}, bf16[2048,1024]{1,0:T(8,128)(2,1)}, u32[]{:S(2)}) %copy-start) | copy-done | bytes 4194328
  145.4 2.2 %copy-done.1 = bf16[2048,1024]{1,0:T(8,128)(2,1)S(1)} copy-done((bf16[2048,1024]{1,0:T(8,128)(2,1)S(1)}, bf16[2048,1024]{1,0:T(8,128)(2,1)}, u32[]{:S(2)}) %copy-start.1) | copy-done | bytes 4194328
  147.6 19.1 %shard_map.100 = (f32[512,1024]{1,0:T(8,128)S(1)}, bf16[512,1024]{1,0:T(8,128)(2,1)S(1)}) custom-call(bf16[512,1024]{1,0:T(8,128)(2,1)S(1)} %bitcast.139, bf16[512,1024]{1,0:T(8,128)(2,1)S(1)} %collective-permute-done.7.peer_ref, bf16[2048,1024]{1,0:T(8,128)(2,1)S(1)} %copy-done.1, bf16[1,2048]{1,0:T(2,128)(2,1)S(1)} %broadcast_in_dim.5.bias_ref, ...), custom_call_target="tpu_custom_call" | custom-call | flops 8589934592 | bytes 8388608 | tf_op jit(solution)/shard_map/pallas_call | solution.py:115
  167.2 2.3 %collective-permute-done.20 = bf16[512,1024]{1,0:T(8,128)(2,1)S(1)} collective-permute-done((bf16[512,1024]{1,0:T(8,128)(2,1)S(1)}, bf16[512,1024]{1,0:T(8,128)(2,1)S(1)}, u32[]{:S(2)}, u32[]{:S(2)}) %collective-permute-start.20) | collective-permute-done | bytes 1048608 | tf_op jit(solution)/shard_map/ppermute | solution.py:172
  170.0 30.7 %all_to_all.32 = bf16[512,4,256]{2,0,1:T(8,128)(2,1)S(1)} all-to-all(bf16[512,4,256]{2,0,1:T(8,128)(2,1)S(1)} %bitcast.142), channel_id=1, replica_groups=mesh['y'=2,'core'=2,'col'=2,'blk'=4] {'blk'}, dimensions={1} | all-to-all | bytes 2097152 | tf_op jit(solution)/shard_map/all_to_all | solution.py:174
  201.8 1.4 add_convert_fusion
  (100 shorter events, 26.2 us)
Async XLA Ops:
  0.0 8.4 %copy-start.2 = (bf16[64,32,256]{2,1,0:T(8,128)(2,1)S(1)}, bf16[64,32,256]{2,1,0:T(8,128)(2,1)}, u32[]{:S(2)}) copy-start(bf16[64,32,256]{2,1,0:T(8,128)(2,1)} %param.10) | copy-start | bytes 3145732
  0.0 11.0 %copy-start.5 = (f32[7,7,256]{2,1,0:T(8,128)S(1)}, f32[7,7,256]{2,1,0:T(8,128)}, u32[]{:S(2)}) copy-start(f32[7,7,256]{2,1,0:T(8,128)} %param.11) | copy-start | bytes 150532
  2.8 54.7 %collective-permute-start.8 = (bf16[272,1024]{1,0:T(8,128)(2,1)}, bf16[272,1024]{1,0:T(8,128)(2,1)}, u32[]{:S(2)}, u32[]{:S(2)}) collective-permute-start(bf16[272,1024]{1,0:T(8,128)(2,1)} %fusion.50), channel_id=1, source_target_pairs={{0,1},{1,2},{2,3},{3,0},{4,5},{5,6},{6,7},{7,4},{8,9},{9,10},{10,1... | collective-permute-start | bytes 1671176 | tf_op jit(solution)/shard_map/ppermute | solution.py:30
  5.8 64.3 %collective-permute-start.12 = (bf16[272,1024]{1,0:T(8,128)(2,1)}, bf16[272,1024]{1,0:T(8,128)(2,1)}, u32[]{:S(2)}, u32[]{:S(2)}) collective-permute-start(bf16[272,1024]{1,0:T(8,128)(2,1)} %fusion.50), channel_id=1, source_target_pairs={{0,2},{1,3},{2,0},{3,1},{4,6},{5,7},{6,4},{7,5},{8,10},{9,11},{10,... | collective-permute-start | bytes 1671176 | tf_op jit(solution)/shard_map/ppermute | solution.py:30
  8.4 3.2 %collective-permute-start = (bf16[3,32,256]{2,1,0:T(8,128)(2,1)S(1)}, bf16[3,32,256]{2,1,0:T(8,128)(2,1)S(1)}, u32[]{:S(2)}, u32[]{:S(2)}) collective-permute-start(bf16[3,32,256]{2,1,0:T(8,128)(2,1)S(1)} %get-tuple-element.16), channel_id=1, source_target_pairs={{0,8},{8,16},{16,24},{1,9},{9,17},{17,25},{2,10},{10,18},{18,26},{... | collective-permute-start | bytes 147464 | tf_op jit(solution)/shard_map/ppermute | solution.py:19
  9.7 4.9 %collective-permute-start.1 = (bf16[3,32,256]{2,1,0:T(8,128)(2,1)S(1)}, bf16[3,32,256]{2,1,0:T(8,128)(2,1)S(1)}, u32[]{:S(2)}, u32[]{:S(2)}) collective-permute-start(bf16[3,32,256]{2,1,0:T(8,128)(2,1)S(1)} %get-tuple-element.15), channel_id=1, source_target_pairs={{8,0},{16,8},{24,16},{9,1},{17,9},{25,17},{10,2},{18,10},{26,18},{... | collective-permute-start | bytes 147464 | tf_op jit(solution)/shard_map/ppermute | solution.py:21
  14.7 6.0 %collective-permute-start.2 = (bf16[70,3,256]{2,1,0:T(4,128)(2,1)S(1)}, bf16[70,3,256]{2,1,0:T(4,128)(2,1)S(1)}, u32[]{:S(2)}, u32[]{:S(2)}) collective-permute-start(bf16[70,3,256]{2,1,0:T(4,128)(2,1)S(1)} %get-tuple-element.13), channel_id=1, source_target_pairs={{0,4},{1,5},{2,6},{3,7},{8,12},{9,13},{10,14},{11,15},{16,20},{17,... | collective-permute-start | bytes 322568 | tf_op jit(solution)/shard_map/ppermute | solution.py:19
  18.1 7.0 %collective-permute-start.3 = (bf16[70,3,256]{2,1,0:T(4,128)(2,1)S(1)}, bf16[70,3,256]{2,1,0:T(4,128)(2,1)S(1)}, u32[]{:S(2)}, u32[]{:S(2)}) collective-permute-start(bf16[70,3,256]{2,1,0:T(4,128)(2,1)S(1)} %get-tuple-element.14), channel_id=1, source_target_pairs={{4,0},{5,1},{6,2},{7,3},{12,8},{13,9},{14,10},{15,11},{20,16},{21,... | collective-permute-start | bytes 322568 | tf_op jit(solution)/shard_map/ppermute | solution.py:21
  42.2 4.6 %copy-start.4 = (bf16[1024,1024]{1,0:T(8,128)(2,1)S(1)}, bf16[1024,1024]{1,0:T(8,128)(2,1)}, u32[]{:S(2)}) copy-start(bf16[1024,1024]{1,0:T(8,128)(2,1)} %param.17) | copy-start | bytes 6291460
  42.9 6.6 %copy-start.10 = (bf16[1024]{0:T(1024)(128)(2,1)S(1)}, bf16[1024]{0:T(1024)(128)(2,1)}, u32[]{:S(2)}) copy-start(bf16[1024]{0:T(1024)(128)(2,1)} %param.16) | copy-start | bytes 6148
  42.9 8.4 %copy-start.6 = (f32[256]{0:T(256)S(1)}, f32[256]{0:T(256)}, u32[]{:S(2)}) copy-start(f32[256]{0:T(256)} %param.14) | copy-start | bytes 3076
  43.0 8.4 %copy-start.7 = (f32[256]{0:T(256)S(1)}, f32[256]{0:T(256)}, u32[]{:S(2)}) copy-start(f32[256]{0:T(256)} %param.13) | copy-start | bytes 3076
  43.0 6.9 %collective-permute-start.4 = (f32[2,64,32]{2,1,0:T(8,128)S(1)}, f32[2,64,32]{2,1,0:T(8,128)S(1)}, u32[]{:S(2)}, u32[]{:S(2)}) collective-permute-start(f32[2,64,32]{2,1,0:T(8,128)S(1)} %pad_maximum_fusion), channel_id=1, source_target_pairs={{0,1},{1,2},{2,3},{3,0},{4,5},{5,6},{6,7},{7,4},{8,9},{9,10},{10,1... | collective-permute-start | bytes 49160 | tf_op jit(solution)/shard_map/ppermute | solution.py:30
  43.2 7.4 %collective-permute-start.5 = (f32[2,64,32]{2,1,0:T(8,128)S(1)}, f32[2,64,32]{2,1,0:T(8,128)S(1)}, u32[]{:S(2)}, u32[]{:S(2)}) collective-permute-start(f32[2,64,32]{2,1,0:T(8,128)S(1)} %pad_maximum_fusion), channel_id=1, source_target_pairs={{0,2},{1,3},{2,0},{3,1},{4,6},{5,7},{6,4},{7,5},{8,10},{9,11},{10,... | collective-permute-start | bytes 49160 | tf_op jit(solution)/shard_map/ppermute | solution.py:30
  44.9 6.4 %collective-permute-start.6 = (f32[2,64,32]{2,1,0:T(8,128)S(1)}, f32[2,64,32]{2,1,0:T(8,128)S(1)}, u32[]{:S(2)}, u32[]{:S(2)}) collective-permute-start(f32[2,64,32]{2,1,0:T(8,128)S(1)} %pad_maximum_fusion), channel_id=1, source_target_pairs={{0,3},{1,0},{2,1},{3,2},{4,7},{5,4},{6,5},{7,6},{8,11},{9,8},{10,9... | collective-permute-start | bytes 49160 | tf_op jit(solution)/shard_map/ppermute | solution.py:30
  49.8 23.4 %collective-permute-start.16 = (bf16[272,1024]{1,0:T(8,128)(2,1)}, bf16[272,1024]{1,0:T(8,128)(2,1)}, u32[]{:S(2)}, u32[]{:S(2)}) collective-permute-start(bf16[272,1024]{1,0:T(8,128)(2,1)} %fusion.50), channel_id=1, source_target_pairs={{0,3},{1,0},{2,1},{3,2},{4,7},{5,4},{6,5},{7,6},{8,11},{9,8},{10,9... | collective-permute-start | bytes 1671176 | tf_op jit(solution)/shard_map/ppermute | solution.py:30
  52.9 81.8 %all-to-all-start = ((bf16[4,512,256]{2,1,0:T(8,128)(2,1)}), bf16[4,512,256]{2,1,0:T(8,128)(2,1)S(1)}, u32[]{:S(2)}, u32[]{:S(2)}) async-start(bf16[4,512,256]{2,1,0:T(8,128)(2,1)} %bitcast.57), calls=%async_computation | async-start | bytes 2097152 | tf_op jit(solution)/shard_map/all_to_all | solution.py:168
  58.3 17.1 %collective-permute-start.9 = (bf16[272,1024]{1,0:T(8,128)(2,1)}, bf16[272,1024]{1,0:T(8,128)(2,1)S(1)}, u32[]{:S(2)}, u32[]{:S(2)}) collective-permute-start(bf16[272,1024]{1,0:T(8,128)(2,1)} %collective-permute-done.8), channel_id=1, source_target_pairs={{0,4},{4,0},{16,20},{20,16},{1,5},{5,1},{17,21},{21,17},{2,6},{6,2... | collective-permute-start | bytes 1671176 | tf_op jit(solution)/shard_map/ppermute | solution.py:66
  58.4 35.7 %collective-permute-start.10 = (bf16[272,1024]{1,0:T(8,128)(2,1)}, bf16[272,1024]{1,0:T(8,128)(2,1)S(1)}, u32[]{:S(2)}, u32[]{:S(2)}) collective-permute-start(bf16[272,1024]{1,0:T(8,128)(2,1)} %collective-permute-done.8), channel_id=1, source_target_pairs={{0,16},{4,20},{16,0},{20,4},{1,17},{5,21},{17,1},{21,5},{2,18},{6,... | collective-permute-start | bytes 1671176 | tf_op jit(solution)/shard_map/ppermute | solution.py:66
  68.7 27.7 %collective-permute-start.11 = (bf16[272,1024]{1,0:T(8,128)(2,1)}, bf16[272,1024]{1,0:T(8,128)(2,1)S(1)}, u32[]{:S(2)}, u32[]{:S(2)}) collective-permute-start(bf16[272,1024]{1,0:T(8,128)(2,1)} %collective-permute-done.8), channel_id=1, source_target_pairs={{0,20},{4,16},{16,4},{20,0},{1,21},{5,17},{17,5},{21,1},{2,22},{6,... | collective-permute-start | bytes 1671176 | tf_op jit(solution)/shard_map/ppermute | solution.py:66
  70.1 27.9 %collective-permute-start.13 = (bf16[272,1024]{1,0:T(8,128)(2,1)}, bf16[272,1024]{1,0:T(8,128)(2,1)S(1)}, u32[]{:S(2)}, u32[]{:S(2)}) collective-permute-start(bf16[272,1024]{1,0:T(8,128)(2,1)} %collective-permute-done.12), channel_id=1, source_target_pairs={{0,4},{4,0},{16,20},{20,16},{1,5},{5,1},{17,21},{21,17},{2,6},{6,2... | collective-permute-start | bytes 1671176 | tf_op jit(solution)/shard_map/ppermute | solution.py:66
  73.2 45.0 %collective-permute-start.14 = (bf16[272,1024]{1,0:T(8,128)(2,1)}, bf16[272,1024]{1,0:T(8,128)(2,1)S(1)}, u32[]{:S(2)}, u32[]{:S(2)}) collective-permute-start(bf16[272,1024]{1,0:T(8,128)(2,1)} %collective-permute-done.12), channel_id=1, source_target_pairs={{0,16},{4,20},{16,0},{20,4},{1,17},{5,21},{17,1},{21,5},{2,18},{6,... | collective-permute-start | bytes 1671176 | tf_op jit(solution)/shard_map/ppermute | solution.py:66
  75.4 43.7 %collective-permute-start.15 = (bf16[272,1024]{1,0:T(8,128)(2,1)}, bf16[272,1024]{1,0:T(8,128)(2,1)S(1)}, u32[]{:S(2)}, u32[]{:S(2)}) collective-permute-start(bf16[272,1024]{1,0:T(8,128)(2,1)} %collective-permute-done.12), channel_id=1, source_target_pairs={{0,20},{4,16},{16,4},{20,0},{1,21},{5,17},{17,5},{21,1},{2,22},{6,... | collective-permute-start | bytes 1671176 | tf_op jit(solution)/shard_map/ppermute | solution.py:66
  94.0 27.8 %collective-permute-start.17 = (bf16[272,1024]{1,0:T(8,128)(2,1)}, bf16[272,1024]{1,0:T(8,128)(2,1)S(1)}, u32[]{:S(2)}, u32[]{:S(2)}) collective-permute-start(bf16[272,1024]{1,0:T(8,128)(2,1)} %collective-permute-done.16), channel_id=1, source_target_pairs={{0,4},{4,0},{16,20},{20,16},{1,5},{5,1},{17,21},{21,17},{2,6},{6,2... | collective-permute-start | bytes 1671176 | tf_op jit(solution)/shard_map/ppermute | solution.py:66
  96.4 36.6 %collective-permute-start.18 = (bf16[272,1024]{1,0:T(8,128)(2,1)}, bf16[272,1024]{1,0:T(8,128)(2,1)S(1)}, u32[]{:S(2)}, u32[]{:S(2)}) collective-permute-start(bf16[272,1024]{1,0:T(8,128)(2,1)} %collective-permute-done.16), channel_id=1, source_target_pairs={{0,16},{4,20},{16,0},{20,4},{1,17},{5,21},{17,1},{21,5},{2,18},{6,... | collective-permute-start | bytes 1671176 | tf_op jit(solution)/shard_map/ppermute | solution.py:66
  97.9 36.9 %collective-permute-start.19 = (bf16[272,1024]{1,0:T(8,128)(2,1)}, bf16[272,1024]{1,0:T(8,128)(2,1)}, u32[]{:S(2)}, u32[]{:S(2)}) collective-permute-start(bf16[272,1024]{1,0:T(8,128)(2,1)} %collective-permute-done.16), channel_id=1, source_target_pairs={{0,20},{4,16},{16,4},{20,0},{1,21},{5,17},{17,5},{21,1},{2,22},{6,... | collective-permute-start | bytes 1671176 | tf_op jit(solution)/shard_map/ppermute | solution.py:66
  134.8 8.4 %collective-permute-start.7 = (bf16[512,1024]{1,0:T(8,128)(2,1)S(1)}, bf16[512,1024]{1,0:T(8,128)(2,1)S(1)}, u32[]{:S(2)}, u32[]{:S(2)}) collective-permute-start(bf16[512,1024]{1,0:T(8,128)(2,1)S(1)} %bitcast.138), channel_id=1, source_target_pairs={{0,8},{8,0},{1,9},{9,1},{2,10},{10,2},{3,11},{11,3},{4,12},{12,4},... | collective-permute-start | bytes 3145736 | tf_op jit(solution)/shard_map/ppermute | solution.py:170
  143.2 2.2 %copy-start = (bf16[2048,1024]{1,0:T(8,128)(2,1)S(1)}, bf16[2048,1024]{1,0:T(8,128)(2,1)}, u32[]{:S(2)}) copy-start(bf16[2048,1024]{1,0:T(8,128)(2,1)} %get-tuple-element.17.second_ref) | copy-start | bytes 12582916
  145.4 2.2 %copy-start.1 = (bf16[2048,1024]{1,0:T(8,128)(2,1)S(1)}, bf16[2048,1024]{1,0:T(8,128)(2,1)}, u32[]{:S(2)}) copy-start(bf16[2048,1024]{1,0:T(8,128)(2,1)} %get-tuple-element.18.first_ref) | copy-start | bytes 12582916
  166.7 2.8 %collective-permute-start.20 = (bf16[512,1024]{1,0:T(8,128)(2,1)S(1)}, bf16[512,1024]{1,0:T(8,128)(2,1)S(1)}, u32[]{:S(2)}, u32[]{:S(2)}) collective-permute-start(bf16[512,1024]{1,0:T(8,128)(2,1)S(1)} %get-tuple-element.8), channel_id=1, source_target_pairs={{0,8},{8,0},{1,9},{9,1},{2,10},{10,2},{3,11},{11,3},{4,12},{12,4},... | collective-permute-start | bytes 3145736 | tf_op jit(solution)/shard_map/ppermute | solution.py:172
  200.6 1.2 copy-start.8
  200.6 1.2 copy-start.9
  (1 other events, 1.2 us)

commit v3 on v2

--- a/solution.py
+++ b/solution.py
@@ -110,7 +110,7 @@
 def mlp_terms(own, peer, w_first, bias, w_second):
     count, chans = own.shape
     hid = w_first.shape[0]
-    tile = min(256, hid)
+    tile = min(512, hid)
     whole = pl.BlockSpec((count, chans), lambda i: (0, 0))
     return pl.pallas_call(
         mlp_kernel,

time: 204 us -> 195 us (0.956)
  Pallas kernels: 19.1 us -> 10.7 us
    pallas_call x1, Pallas kernels: 19.1 us -> 10.7 us  [mlp_terms(): pl.pallas_call(mlp_kernel, grid=(hid // tile,), in_specs=[whole, whole, p...]
  transfers between devices with their start and end apart: 22 -> 22, of which waited for: 10 -> 10; matrix products, arithmetic and copies ran while one was open for 21% -> 22% of each run, Pallas kernels for 0% -> 0%
where the time goes in v3:
time: 195 us
  starting transfers between devices  57.8 us (30%)
  waiting for transfers between devices  42.2 us (22%)
  local copies, waits for them, and re-layouts  31.1 us (16%)
  blocking collectives  30.6 us (16%)
  other arithmetic  22.1 us (11%)
  Pallas kernels  10.7 us (5%)
    ppermute x9, starting transfers between devices, passed(): lax.ppermute(arrived, ('y', 'col'), [(i, i ^ j) for i in range(plane)])  35 us
    ppermute x9, waiting for transfers between devices, passed(): lax.ppermute(arrived, ('y', 'col'), [(i, i ^ j) for i in range(plane)])  31.3 us
    all_to_all x1, blocking collectives, shards(): summed = lax.all_to_all(mlp, 'blk', split_axis=1, concat_axis=0, tiled=True)  30.6 us
    unnamed x48, local copies, waits for them, and re-layouts  22.9 us
    reduce_sum x1, other arithmetic, shards(): part_mean = jnp.mean(conv_out, axis=-1)  16.5 us
    pallas_call x1, Pallas kernels, mlp_terms(): pl.pallas_call(mlp_kernel, grid=(hid // tile,), in_specs=[whole, whole, p...  10.7 us
    ppermute x6, starting transfers between devices, rotated(): lax.ppermute(value, 'blk', [(i, (i + shift) % count) for i in range(count)])  10.3 us
    ppermute x2, waiting for transfers between devices, with_halo(): lax.ppermute(head, axis, [((i + 1) % count, i) for i in range(ends)])  7.24 us
  transfers between devices with their start and end apart: 22, of which 10 were waited for; matrix products, arithmetic and copies ran while one was open for 22% of the time, Pallas kernels for 0%

profile of v3, /device:TPU:0, one launch (start us, length us, event | category | flops | bytes accessed | tf_op | source)
XLA Modules:
  0.0 194.8 jit_solution(9113327738865590035)
XLA Ops:
  2.8 3.0 %collective-permute-start.8 = (bf16[272,1024]{1,0:T(8,128)(2,1)}, bf16[272,1024]{1,0:T(8,128)(2,1)}, u32[]{:S(2)}, u32[]{:S(2)}) collective-permute-start(bf16[272,1024]{1,0:T(8,128)(2,1)} %fusion.50), channel_id=1, source_target_pairs={{0,1},{1,2},{2,3},{3,0},{4,5},{5,6},{6,7},{7,4},{8,9},{9,10},{10,1... | collective-permute-start | bytes 1671176 | tf_op jit(solution)/shard_map/ppermute | solution.py:30
  5.8 2.6 %collective-permute-start.12 = (bf16[272,1024]{1,0:T(8,128)(2,1)}, bf16[272,1024]{1,0:T(8,128)(2,1)}, u32[]{:S(2)}, u32[]{:S(2)}) collective-permute-start(bf16[272,1024]{1,0:T(8,128)(2,1)} %fusion.50), channel_id=1, source_target_pairs={{0,2},{1,3},{2,0},{3,1},{4,6},{5,7},{6,4},{7,5},{8,10},{9,11},{10,... | collective-permute-start | bytes 1671176 | tf_op jit(solution)/shard_map/ppermute | solution.py:30
  8.4 1.3 collective-permute-start
  11.7 2.9 %collective-permute-done.1 = bf16[3,32,256]{2,1,0:T(8,128)(2,1)S(1)} collective-permute-done((bf16[3,32,256]{2,1,0:T(8,128)(2,1)S(1)}, bf16[3,32,256]{2,1,0:T(8,128)(2,1)S(1)}, u32[]{:S(2)}, u32[]{:S(2)}) %collective-permute-start.1) | collective-permute-done | bytes 49184 | tf_op jit(solution)/shard_map/ppermute | solution.py:21
  14.7 3.4 %collective-permute-start.2 = (bf16[70,3,256]{2,1,0:T(4,128)(2,1)S(1)}, bf16[70,3,256]{2,1,0:T(4,128)(2,1)S(1)}, u32[]{:S(2)}, u32[]{:S(2)}) collective-permute-start(bf16[70,3,256]{2,1,0:T(4,128)(2,1)S(1)} %get-tuple-element.13), channel_id=1, source_target_pairs={{0,4},{1,5},{2,6},{3,7},{8,12},{9,13},{10,14},{11,15},{16,20},{17,... | collective-permute-start | bytes 322568 | tf_op jit(solution)/shard_map/ppermute | solution.py:19
  20.7 4.4 %collective-permute-done.3 = bf16[70,3,256]{2,1,0:T(4,128)(2,1)S(1)} collective-permute-done((bf16[70,3,256]{2,1,0:T(4,128)(2,1)S(1)}, bf16[70,3,256]{2,1,0:T(4,128)(2,1)S(1)}, u32[]{:S(2)}, u32[]{:S(2)}) %collective-permute-start.3) | collective-permute-done | bytes 107552 | tf_op jit(solution)/shard_map/ppermute | solution.py:21
  25.7 16.5 %fusion.61 = (f32[64,32]{1,0:T(8,128)S(1)}, f32[64,32,256]{2,1,0:T(8,128)S(1)}) fusion(f32[256]{0:T(256)} %bitcast.192, f32[70,38,256]{2,1,0:T(8,128)S(1)} %maximum_convert_fusion, f32[256]{0:T(256)} %bitcast.193, f32[256]{0:T(256)S(1)} %bitcast.146, f32[256]{0:T(256)S(1)} %bitcast.147, f32[256]{0:T(256)S(1)} %bitcast.148, f32[256]{0:T(256)S(1)} %bitcast.149, ...), kind=kLoop, calls=%fused_computation.170 | loop fusion | flops 51902464 | bytes 104916992 | tf_op jit(solution)/shard_map/reduce_sum | solution.py:154
  43.2 1.7 collective-permute-start.5
  44.9 1.9 collective-permute-start.6
  46.9 2.7 %dynamic-slice_dynamic-update-slice_fusion = (bf16[2048,1024]{1,0:T(8,128)(2,1)}, bf16[2048,1024]{1,0:T(8,128)(2,1)}) fusion(bf16[1024,1024]{1,0:T(8,128)(2,1)S(1)} %copy-done.4, s32[]{:T(128)S(6)} %select_n.4, bf16[1024,1024]{1,0:T(8,128)(2,1)} %param.15), kind=kLoop, calls=%fused_computation.106 | loop fusion | bytes 4194308
  51.4 1.5 add_convert_fusion.2
  52.9 4.6 %all-to-all-start = ((bf16[4,512,256]{2,1,0:T(8,128)(2,1)}), bf16[4,512,256]{2,1,0:T(8,128)(2,1)S(1)}, u32[]{:S(2)}, u32[]{:S(2)}) async-start(bf16[4,512,256]{2,1,0:T(8,128)(2,1)} %bitcast.57), calls=%async_computation | async-start | bytes 2097152 | tf_op jit(solution)/shard_map/all_to_all | solution.py:168
  58.4 10.3 %collective-permute-start.10 = (bf16[272,1024]{1,0:T(8,128)(2,1)}, bf16[272,1024]{1,0:T(8,128)(2,1)S(1)}, u32[]{:S(2)}, u32[]{:S(2)}) collective-permute-start(bf16[272,1024]{1,0:T(8,128)(2,1)} %collective-permute-done.8), channel_id=1, source_target_pairs={{0,16},{4,20},{16,0},{20,4},{1,17},{5,21},{17,1},{21,5},{2,18},{6,... | collective-permute-start | bytes 1671176 | tf_op jit(solution)/shard_map/ppermute | solution.py:66
  68.7 1.4 collective-permute-start.11
  71.4 1.9 slice_dynamic-update-slice_fusion.11
  73.2 1.5 collective-permute-start.14
  75.4 8.4 %collective-permute-start.15 = (bf16[272,1024]{1,0:T(8,128)(2,1)}, bf16[272,1024]{1,0:T(8,128)(2,1)S(1)}, u32[]{:S(2)}, u32[]{:S(2)}) collective-permute-start(bf16[272,1024]{1,0:T(8,128)(2,1)} %collective-permute-done.12), channel_id=1, source_target_pairs={{0,20},{4,16},{16,4},{20,0},{1,21},{5,17},{17,5},{21,1},{2,22},{6,... | collective-permute-start | bytes 1671176 | tf_op jit(solution)/shard_map/ppermute | solution.py:66
  84.7 9.4 %collective-permute-done.10 = bf16[272,1024]{1,0:T(8,128)(2,1)S(1)} collective-permute-done((bf16[272,1024]{1,0:T(8,128)(2,1)}, bf16[272,1024]{1,0:T(8,128)(2,1)S(1)}, u32[]{:S(2)}, u32[]{:S(2)}) %collective-permute-start.10) | collective-permute-done | bytes 557088 | tf_op jit(solution)/shard_map/ppermute | solution.py:66
  94.0 2.3 %collective-permute-start.17 = (bf16[272,1024]{1,0:T(8,128)(2,1)}, bf16[272,1024]{1,0:T(8,128)(2,1)S(1)}, u32[]{:S(2)}, u32[]{:S(2)}) collective-permute-start(bf16[272,1024]{1,0:T(8,128)(2,1)} %collective-permute-done.16), channel_id=1, source_target_pairs={{0,4},{4,0},{16,20},{20,16},{1,5},{5,1},{17,21},{21,17},{2,6},{6,2... | collective-permute-start | bytes 1671176 | tf_op jit(solution)/shard_map/ppermute | solution.py:66
  97.9 9.8 %collective-permute-start.19 = (bf16[272,1024]{1,0:T(8,128)(2,1)}, bf16[272,1024]{1,0:T(8,128)(2,1)}, u32[]{:S(2)}, u32[]{:S(2)}) collective-permute-start(bf16[272,1024]{1,0:T(8,128)(2,1)} %collective-permute-done.16), channel_id=1, source_target_pairs={{0,20},{4,16},{16,4},{20,0},{1,21},{5,17},{17,5},{21,1},{2,22},{6,... | collective-permute-start | bytes 1671176 | tf_op jit(solution)/shard_map/ppermute | solution.py:66
  107.7 10.5 %collective-permute-done.14 = bf16[272,1024]{1,0:T(8,128)(2,1)S(1)} collective-permute-done((bf16[272,1024]{1,0:T(8,128)(2,1)}, bf16[272,1024]{1,0:T(8,128)(2,1)S(1)}, u32[]{:S(2)}, u32[]{:S(2)}) %collective-permute-start.14) | collective-permute-done | bytes 557088 | tf_op jit(solution)/shard_map/ppermute | solution.py:66
  119.1 2.8 %collective-permute-done.17 = bf16[272,1024]{1,0:T(8,128)(2,1)S(1)} collective-permute-done((bf16[272,1024]{1,0:T(8,128)(2,1)}, bf16[272,1024]{1,0:T(8,128)(2,1)S(1)}, u32[]{:S(2)}, u32[]{:S(2)}) %collective-permute-start.17) | collective-permute-done | bytes 557088 | tf_op jit(solution)/shard_map/ppermute | solution.py:66
  121.9 1.9 slice_dynamic-update-slice_fusion.7
  124.5 8.5 %collective-permute-done.18 = bf16[272,1024]{1,0:T(8,128)(2,1)S(1)} collective-permute-done((bf16[272,1024]{1,0:T(8,128)(2,1)}, bf16[272,1024]{1,0:T(8,128)(2,1)S(1)}, u32[]{:S(2)}, u32[]{:S(2)}) %collective-permute-start.18) | collective-permute-done | bytes 557088 | tf_op jit(solution)/shard_map/ppermute | solution.py:66
  137.7 1.9 slice_dynamic-update-slice_fusion.3
  141.3 1.9 slice_dynamic-update-slice_fusion
  143.2 2.2 %copy-done = bf16[2048,1024]{1,0:T(8,128)(2,1)S(1)} copy-done((bf16[2048,1024]{1,0:T(8,128)(2,1)S(1)}, bf16[2048,1024]{1,0:T(8,128)(2,1)}, u32[]{:S(2)}) %copy-start) | copy-done | bytes 4194328
  145.4 2.2 %copy-done.1 = bf16[2048,1024]{1,0:T(8,128)(2,1)S(1)} copy-done((bf16[2048,1024]{1,0:T(8,128)(2,1)S(1)}, bf16[2048,1024]{1,0:T(8,128)(2,1)}, u32[]{:S(2)}) %copy-start.1) | copy-done | bytes 4194328
  147.6 10.7 %shard_map.100 = (f32[512,1024]{1,0:T(8,128)S(1)}, bf16[512,1024]{1,0:T(8,128)(2,1)S(1)}) custom-call(bf16[512,1024]{1,0:T(8,128)(2,1)S(1)} %bitcast.139, bf16[512,1024]{1,0:T(8,128)(2,1)S(1)} %collective-permute-done.7.peer_ref, bf16[2048,1024]{1,0:T(8,128)(2,1)S(1)} %copy-done.1, bf16[1,2048]{1,0:T(2,128)(2,1)S(1)} %broadcast_in_dim.5.bias_ref, ...), custom_call_target="tpu_custom_call" | custom-call | flops 8589934592 | bytes 8388608 | tf_op jit(solution)/shard_map/pallas_call | solution.py:115
  158.8 2.3 %collective-permute-done.20 = bf16[512,1024]{1,0:T(8,128)(2,1)S(1)} collective-permute-done((bf16[512,1024]{1,0:T(8,128)(2,1)S(1)}, bf16[512,1024]{1,0:T(8,128)(2,1)S(1)}, u32[]{:S(2)}, u32[]{:S(2)}) %collective-permute-start.20) | collective-permute-done | bytes 1048608 | tf_op jit(solution)/shard_map/ppermute | solution.py:172
  161.6 30.6 %all_to_all.32 = bf16[512,4,256]{2,0,1:T(8,128)(2,1)S(1)} all-to-all(bf16[512,4,256]{2,0,1:T(8,128)(2,1)S(1)} %bitcast.142), channel_id=1, replica_groups=mesh['y'=2,'core'=2,'col'=2,'blk'=4] {'blk'}, dimensions={1} | all-to-all | bytes 2097152 | tf_op jit(solution)/shard_map/all_to_all | solution.py:174
  193.4 1.4 add_convert_fusion
  (100 shorter events, 26.2 us)
Async XLA Ops:
  0.0 8.4 %copy-start.2 = (bf16[64,32,256]{2,1,0:T(8,128)(2,1)S(1)}, bf16[64,32,256]{2,1,0:T(8,128)(2,1)}, u32[]{:S(2)}) copy-start(bf16[64,32,256]{2,1,0:T(8,128)(2,1)} %param.10) | copy-start | bytes 3145732
  0.0 11.0 %copy-start.5 = (f32[7,7,256]{2,1,0:T(8,128)S(1)}, f32[7,7,256]{2,1,0:T(8,128)}, u32[]{:S(2)}) copy-start(f32[7,7,256]{2,1,0:T(8,128)} %param.11) | copy-start | bytes 150532
  2.8 54.7 %collective-permute-start.8 = (bf16[272,1024]{1,0:T(8,128)(2,1)}, bf16[272,1024]{1,0:T(8,128)(2,1)}, u32[]{:S(2)}, u32[]{:S(2)}) collective-permute-start(bf16[272,1024]{1,0:T(8,128)(2,1)} %fusion.50), channel_id=1, source_target_pairs={{0,1},{1,2},{2,3},{3,0},{4,5},{5,6},{6,7},{7,4},{8,9},{9,10},{10,1... | collective-permute-start | bytes 1671176 | tf_op jit(solution)/shard_map/ppermute | solution.py:30
  5.8 64.3 %collective-permute-start.12 = (bf16[272,1024]{1,0:T(8,128)(2,1)}, bf16[272,1024]{1,0:T(8,128)(2,1)}, u32[]{:S(2)}, u32[]{:S(2)}) collective-permute-start(bf16[272,1024]{1,0:T(8,128)(2,1)} %fusion.50), channel_id=1, source_target_pairs={{0,2},{1,3},{2,0},{3,1},{4,6},{5,7},{6,4},{7,5},{8,10},{9,11},{10,... | collective-permute-start | bytes 1671176 | tf_op jit(solution)/shard_map/ppermute | solution.py:30
  8.4 3.2 %collective-permute-start = (bf16[3,32,256]{2,1,0:T(8,128)(2,1)S(1)}, bf16[3,32,256]{2,1,0:T(8,128)(2,1)S(1)}, u32[]{:S(2)}, u32[]{:S(2)}) collective-permute-start(bf16[3,32,256]{2,1,0:T(8,128)(2,1)S(1)} %get-tuple-element.16), channel_id=1, source_target_pairs={{0,8},{8,16},{16,24},{1,9},{9,17},{17,25},{2,10},{10,18},{18,26},{... | collective-permute-start | bytes 147464 | tf_op jit(solution)/shard_map/ppermute | solution.py:19
  9.7 4.9 %collective-permute-start.1 = (bf16[3,32,256]{2,1,0:T(8,128)(2,1)S(1)}, bf16[3,32,256]{2,1,0:T(8,128)(2,1)S(1)}, u32[]{:S(2)}, u32[]{:S(2)}) collective-permute-start(bf16[3,32,256]{2,1,0:T(8,128)(2,1)S(1)} %get-tuple-element.15), channel_id=1, source_target_pairs={{8,0},{16,8},{24,16},{9,1},{17,9},{25,17},{10,2},{18,10},{26,18},{... | collective-permute-start | bytes 147464 | tf_op jit(solution)/shard_map/ppermute | solution.py:21
  14.7 6.0 %collective-permute-start.2 = (bf16[70,3,256]{2,1,0:T(4,128)(2,1)S(1)}, bf16[70,3,256]{2,1,0:T(4,128)(2,1)S(1)}, u32[]{:S(2)}, u32[]{:S(2)}) collective-permute-start(bf16[70,3,256]{2,1,0:T(4,128)(2,1)S(1)} %get-tuple-element.13), channel_id=1, source_target_pairs={{0,4},{1,5},{2,6},{3,7},{8,12},{9,13},{10,14},{11,15},{16,20},{17,... | collective-permute-start | bytes 322568 | tf_op jit(solution)/shard_map/ppermute | solution.py:19
  18.1 7.0 %collective-permute-start.3 = (bf16[70,3,256]{2,1,0:T(4,128)(2,1)S(1)}, bf16[70,3,256]{2,1,0:T(4,128)(2,1)S(1)}, u32[]{:S(2)}, u32[]{:S(2)}) collective-permute-start(bf16[70,3,256]{2,1,0:T(4,128)(2,1)S(1)} %get-tuple-element.14), channel_id=1, source_target_pairs={{4,0},{5,1},{6,2},{7,3},{12,8},{13,9},{14,10},{15,11},{20,16},{21,... | collective-permute-start | bytes 322568 | tf_op jit(solution)/shard_map/ppermute | solution.py:21
  42.2 4.6 %copy-start.4 = (bf16[1024,1024]{1,0:T(8,128)(2,1)S(1)}, bf16[1024,1024]{1,0:T(8,128)(2,1)}, u32[]{:S(2)}) copy-start(bf16[1024,1024]{1,0:T(8,128)(2,1)} %param.17) | copy-start | bytes 6291460
  42.9 6.6 %copy-start.10 = (bf16[1024]{0:T(1024)(128)(2,1)S(1)}, bf16[1024]{0:T(1024)(128)(2,1)}, u32[]{:S(2)}) copy-start(bf16[1024]{0:T(1024)(128)(2,1)} %param.16) | copy-start | bytes 6148
  42.9 8.4 %copy-start.6 = (f32[256]{0:T(256)S(1)}, f32[256]{0:T(256)}, u32[]{:S(2)}) copy-start(f32[256]{0:T(256)} %param.14) | copy-start | bytes 3076
  43.0 8.4 %copy-start.7 = (f32[256]{0:T(256)S(1)}, f32[256]{0:T(256)}, u32[]{:S(2)}) copy-start(f32[256]{0:T(256)} %param.13) | copy-start | bytes 3076
  43.0 6.9 %collective-permute-start.4 = (f32[2,64,32]{2,1,0:T(8,128)S(1)}, f32[2,64,32]{2,1,0:T(8,128)S(1)}, u32[]{:S(2)}, u32[]{:S(2)}) collective-permute-start(f32[2,64,32]{2,1,0:T(8,128)S(1)} %pad_maximum_fusion), channel_id=1, source_target_pairs={{0,1},{1,2},{2,3},{3,0},{4,5},{5,6},{6,7},{7,4},{8,9},{9,10},{10,1... | collective-permute-start | bytes 49160 | tf_op jit(solution)/shard_map/ppermute | solution.py:30
  43.2 7.4 %collective-permute-start.5 = (f32[2,64,32]{2,1,0:T(8,128)S(1)}, f32[2,64,32]{2,1,0:T(8,128)S(1)}, u32[]{:S(2)}, u32[]{:S(2)}) collective-permute-start(f32[2,64,32]{2,1,0:T(8,128)S(1)} %pad_maximum_fusion), channel_id=1, source_target_pairs={{0,2},{1,3},{2,0},{3,1},{4,6},{5,7},{6,4},{7,5},{8,10},{9,11},{10,... | collective-permute-start | bytes 49160 | tf_op jit(solution)/shard_map/ppermute | solution.py:30
  44.9 6.4 %collective-permute-start.6 = (f32[2,64,32]{2,1,0:T(8,128)S(1)}, f32[2,64,32]{2,1,0:T(8,128)S(1)}, u32[]{:S(2)}, u32[]{:S(2)}) collective-permute-start(f32[2,64,32]{2,1,0:T(8,128)S(1)} %pad_maximum_fusion), channel_id=1, source_target_pairs={{0,3},{1,0},{2,1},{3,2},{4,7},{5,4},{6,5},{7,6},{8,11},{9,8},{10,9... | collective-permute-start | bytes 49160 | tf_op jit(solution)/shard_map/ppermute | solution.py:30
  49.8 23.4 %collective-permute-start.16 = (bf16[272,1024]{1,0:T(8,128)(2,1)}, bf16[272,1024]{1,0:T(8,128)(2,1)}, u32[]{:S(2)}, u32[]{:S(2)}) collective-permute-start(bf16[272,1024]{1,0:T(8,128)(2,1)} %fusion.50), channel_id=1, source_target_pairs={{0,3},{1,0},{2,1},{3,2},{4,7},{5,4},{6,5},{7,6},{8,11},{9,8},{10,9... | collective-permute-start | bytes 1671176 | tf_op jit(solution)/shard_map/ppermute | solution.py:30
  52.9 81.8 %all-to-all-start = ((bf16[4,512,256]{2,1,0:T(8,128)(2,1)}), bf16[4,512,256]{2,1,0:T(8,128)(2,1)S(1)}, u32[]{:S(2)}, u32[]{:S(2)}) async-start(bf16[4,512,256]{2,1,0:T(8,128)(2,1)} %bitcast.57), calls=%async_computation | async-start | bytes 2097152 | tf_op jit(solution)/shard_map/all_to_all | solution.py:168
  58.3 17.1 %collective-permute-start.9 = (bf16[272,1024]{1,0:T(8,128)(2,1)}, bf16[272,1024]{1,0:T(8,128)(2,1)S(1)}, u32[]{:S(2)}, u32[]{:S(2)}) collective-permute-start(bf16[272,1024]{1,0:T(8,128)(2,1)} %collective-permute-done.8), channel_id=1, source_target_pairs={{0,4},{4,0},{16,20},{20,16},{1,5},{5,1},{17,21},{21,17},{2,6},{6,2... | collective-permute-start | bytes 1671176 | tf_op jit(solution)/shard_map/ppermute | solution.py:66
  58.4 35.7 %collective-permute-start.10 = (bf16[272,1024]{1,0:T(8,128)(2,1)}, bf16[272,1024]{1,0:T(8,128)(2,1)S(1)}, u32[]{:S(2)}, u32[]{:S(2)}) collective-permute-start(bf16[272,1024]{1,0:T(8,128)(2,1)} %collective-permute-done.8), channel_id=1, source_target_pairs={{0,16},{4,20},{16,0},{20,4},{1,17},{5,21},{17,1},{21,5},{2,18},{6,... | collective-permute-start | bytes 1671176 | tf_op jit(solution)/shard_map/ppermute | solution.py:66
  68.7 27.7 %collective-permute-start.11 = (bf16[272,1024]{1,0:T(8,128)(2,1)}, bf16[272,1024]{1,0:T(8,128)(2,1)S(1)}, u32[]{:S(2)}, u32[]{:S(2)}) collective-permute-start(bf16[272,1024]{1,0:T(8,128)(2,1)} %collective-permute-done.8), channel_id=1, source_target_pairs={{0,20},{4,16},{16,4},{20,0},{1,21},{5,17},{17,5},{21,1},{2,22},{6,... | collective-permute-start | bytes 1671176 | tf_op jit(solution)/shard_map/ppermute | solution.py:66
  70.1 27.9 %collective-permute-start.13 = (bf16[272,1024]{1,0:T(8,128)(2,1)}, bf16[272,1024]{1,0:T(8,128)(2,1)S(1)}, u32[]{:S(2)}, u32[]{:S(2)}) collective-permute-start(bf16[272,1024]{1,0:T(8,128)(2,1)} %collective-permute-done.12), channel_id=1, source_target_pairs={{0,4},{4,0},{16,20},{20,16},{1,5},{5,1},{17,21},{21,17},{2,6},{6,2... | collective-permute-start | bytes 1671176 | tf_op jit(solution)/shard_map/ppermute | solution.py:66
  73.2 45.0 %collective-permute-start.14 = (bf16[272,1024]{1,0:T(8,128)(2,1)}, bf16[272,1024]{1,0:T(8,128)(2,1)S(1)}, u32[]{:S(2)}, u32[]{:S(2)}) collective-permute-start(bf16[272,1024]{1,0:T(8,128)(2,1)} %collective-permute-done.12), channel_id=1, source_target_pairs={{0,16},{4,20},{16,0},{20,4},{1,17},{5,21},{17,1},{21,5},{2,18},{6,... | collective-permute-start | bytes 1671176 | tf_op jit(solution)/shard_map/ppermute | solution.py:66
  75.4 43.7 %collective-permute-start.15 = (bf16[272,1024]{1,0:T(8,128)(2,1)}, bf16[272,1024]{1,0:T(8,128)(2,1)S(1)}, u32[]{:S(2)}, u32[]{:S(2)}) collective-permute-start(bf16[272,1024]{1,0:T(8,128)(2,1)} %collective-permute-done.12), channel_id=1, source_target_pairs={{0,20},{4,16},{16,4},{20,0},{1,21},{5,17},{17,5},{21,1},{2,22},{6,... | collective-permute-start | bytes 1671176 | tf_op jit(solution)/shard_map/ppermute | solution.py:66
  94.0 27.8 %collective-permute-start.17 = (bf16[272,1024]{1,0:T(8,128)(2,1)}, bf16[272,1024]{1,0:T(8,128)(2,1)S(1)}, u32[]{:S(2)}, u32[]{:S(2)}) collective-permute-start(bf16[272,1024]{1,0:T(8,128)(2,1)} %collective-permute-done.16), channel_id=1, source_target_pairs={{0,4},{4,0},{16,20},{20,16},{1,5},{5,1},{17,21},{21,17},{2,6},{6,2... | collective-permute-start | bytes 1671176 | tf_op jit(solution)/shard_map/ppermute | solution.py:66
  96.4 36.6 %collective-permute-start.18 = (bf16[272,1024]{1,0:T(8,128)(2,1)}, bf16[272,1024]{1,0:T(8,128)(2,1)S(1)}, u32[]{:S(2)}, u32[]{:S(2)}) collective-permute-start(bf16[272,1024]{1,0:T(8,128)(2,1)} %collective-permute-done.16), channel_id=1, source_target_pairs={{0,16},{4,20},{16,0},{20,4},{1,17},{5,21},{17,1},{21,5},{2,18},{6,... | collective-permute-start | bytes 1671176 | tf_op jit(solution)/shard_map/ppermute | solution.py:66
  97.9 36.9 %collective-permute-start.19 = (bf16[272,1024]{1,0:T(8,128)(2,1)}, bf16[272,1024]{1,0:T(8,128)(2,1)}, u32[]{:S(2)}, u32[]{:S(2)}) collective-permute-start(bf16[272,1024]{1,0:T(8,128)(2,1)} %collective-permute-done.16), channel_id=1, source_target_pairs={{0,20},{4,16},{16,4},{20,0},{1,21},{5,17},{17,5},{21,1},{2,22},{6,... | collective-permute-start | bytes 1671176 | tf_op jit(solution)/shard_map/ppermute | solution.py:66
  134.8 8.4 %collective-permute-start.7 = (bf16[512,1024]{1,0:T(8,128)(2,1)S(1)}, bf16[512,1024]{1,0:T(8,128)(2,1)S(1)}, u32[]{:S(2)}, u32[]{:S(2)}) collective-permute-start(bf16[512,1024]{1,0:T(8,128)(2,1)S(1)} %bitcast.138), channel_id=1, source_target_pairs={{0,8},{8,0},{1,9},{9,1},{2,10},{10,2},{3,11},{11,3},{4,12},{12,4},... | collective-permute-start | bytes 3145736 | tf_op jit(solution)/shard_map/ppermute | solution.py:170
  143.2 2.2 %copy-start = (bf16[2048,1024]{1,0:T(8,128)(2,1)S(1)}, bf16[2048,1024]{1,0:T(8,128)(2,1)}, u32[]{:S(2)}) copy-start(bf16[2048,1024]{1,0:T(8,128)(2,1)} %get-tuple-element.17.second_ref) | copy-start | bytes 12582916
  145.4 2.2 %copy-start.1 = (bf16[2048,1024]{1,0:T(8,128)(2,1)S(1)}, bf16[2048,1024]{1,0:T(8,128)(2,1)}, u32[]{:S(2)}) copy-start(bf16[2048,1024]{1,0:T(8,128)(2,1)} %get-tuple-element.18.first_ref) | copy-start | bytes 12582916
  158.3 2.8 %collective-permute-start.20 = (bf16[512,1024]{1,0:T(8,128)(2,1)S(1)}, bf16[512,1024]{1,0:T(8,128)(2,1)S(1)}, u32[]{:S(2)}, u32[]{:S(2)}) collective-permute-start(bf16[512,1024]{1,0:T(8,128)(2,1)S(1)} %get-tuple-element.8), channel_id=1, source_target_pairs={{0,8},{8,0},{1,9},{9,1},{2,10},{10,2},{3,11},{11,3},{4,12},{12,4},... | collective-permute-start | bytes 3145736 | tf_op jit(solution)/shard_map/ppermute | solution.py:172
  192.2 1.2 copy-start.8
  192.2 1.2 copy-start.9
  (1 other events, 1.2 us)

commit v4 on v3

--- a/solution.py
+++ b/solution.py
@@ -110,7 +110,7 @@
 def mlp_terms(own, peer, w_first, bias, w_second):
     count, chans = own.shape
     hid = w_first.shape[0]
-    tile = min(512, hid)
+    tile = min(1024, hid)
     whole = pl.BlockSpec((count, chans), lambda i: (0, 0))
     return pl.pallas_call(
         mlp_kernel,
@@ -128,7 +128,7 @@
             jax.ShapeDtypeStruct((count, chans), jnp.bfloat16),
         ],
         scratch_shapes=[pltpu.VMEM((count, chans), jnp.float32)],
-        compiler_params=pltpu.CompilerParams(vmem_limit_bytes=32 * 1024 * 1024),
+        compiler_params=pltpu.CompilerParams(vmem_limit_bytes=48 * 1024 * 1024),
         cost_estimate=pl.CostEstimate(
             flops=8 * count * chans * hid, bytes_accessed=16 * count * chans, transcendentals=0
         ),

time: 195 us -> 192 us (0.985)
  local copies, waits for them, and re-layouts: 31.1 us -> 26.8 us
    unnamed x48 -> x44, local copies, waits for them, and re-layouts: 22.9 us -> 18.4 us
where the time goes in v4:
time: 192 us
  starting transfers between devices  57.8 us (30%)
  waiting for transfers between devices  42.2 us (22%)
  blocking collectives  30.7 us (16%)
  local copies, waits for them, and re-layouts  26.8 us (14%)
  other arithmetic  22.1 us (12%)
  Pallas kernels  11.9 us (6%)
    ppermute x9, starting transfers between devices, passed(): lax.ppermute(arrived, ('y', 'col'), [(i, i ^ j) for i in range(plane)])  34.9 us
    ppermute x9, waiting for transfers between devices, passed(): lax.ppermute(arrived, ('y', 'col'), [(i, i ^ j) for i in range(plane)])  31.3 us
    all_to_all x1, blocking collectives, shards(): summed = lax.all_to_all(mlp, 'blk', split_axis=1, concat_axis=0, tiled=True)  30.7 us
    unnamed x44, local copies, waits for them, and re-layouts  18.4 us
    reduce_sum x1, other arithmetic, shards(): part_mean = jnp.mean(conv_out, axis=-1)  16.5 us
    pallas_call x1, Pallas kernels, mlp_terms(): pl.pallas_call(mlp_kernel, grid=(hid // tile,), in_specs=[whole, whole, p...  11.9 us
    ppermute x6, starting transfers between devices, rotated(): lax.ppermute(value, 'blk', [(i, (i + shift) % count) for i in range(count)])  10.3 us
    ppermute x2, waiting for transfers between devices, with_halo(): lax.ppermute(head, axis, [((i + 1) % count, i) for i in range(ends)])  7.22 us
  transfers between devices with their start and end apart: 22, of which 10 were waited for; matrix products, arithmetic and copies ran while one was open for 22% of the time, Pallas kernels for 0%

profile of v4, /device:TPU:0, one launch (start us, length us, event | category | flops | bytes accessed | tf_op | source)
XLA Modules:
  0.0 191.7 jit_solution(2033555783639800869)
XLA Ops:
  2.8 3.0 %collective-permute-start.8 = (bf16[272,1024]{1,0:T(8,128)(2,1)}, bf16[272,1024]{1,0:T(8,128)(2,1)}, u32[]{:S(2)}, u32[]{:S(2)}) collective-permute-start(bf16[272,1024]{1,0:T(8,128)(2,1)} %fusion.50), channel_id=1, source_target_pairs={{0,1},{1,2},{2,3},{3,0},{4,5},{5,6},{6,7},{7,4},{8,9},{9,10},{10,1... | collective-permute-start | bytes 1671176 | tf_op jit(solution)/shard_map/ppermute | solution.py:30
  5.8 2.6 %collective-permute-start.12 = (bf16[272,1024]{1,0:T(8,128)(2,1)}, bf16[272,1024]{1,0:T(8,128)(2,1)}, u32[]{:S(2)}, u32[]{:S(2)}) collective-permute-start(bf16[272,1024]{1,0:T(8,128)(2,1)} %fusion.50), channel_id=1, source_target_pairs={{0,2},{1,3},{2,0},{3,1},{4,6},{5,7},{6,4},{7,5},{8,10},{9,11},{10,... | collective-permute-start | bytes 1671176 | tf_op jit(solution)/shard_map/ppermute | solution.py:30
  8.4 1.3 collective-permute-start
  9.7 1.3 collective-permute-start.1
  11.7 2.8 %collective-permute-done.1 = bf16[3,32,256]{2,1,0:T(8,128)(2,1)S(1)} collective-permute-done((bf16[3,32,256]{2,1,0:T(8,128)(2,1)S(1)}, bf16[3,32,256]{2,1,0:T(8,128)(2,1)S(1)}, u32[]{:S(2)}, u32[]{:S(2)}) %collective-permute-start.1) | collective-permute-done | bytes 49184 | tf_op jit(solution)/shard_map/ppermute | solution.py:21
  14.7 3.4 %collective-permute-start.2 = (bf16[70,3,256]{2,1,0:T(4,128)(2,1)S(1)}, bf16[70,3,256]{2,1,0:T(4,128)(2,1)S(1)}, u32[]{:S(2)}, u32[]{:S(2)}) collective-permute-start(bf16[70,3,256]{2,1,0:T(4,128)(2,1)S(1)} %get-tuple-element.13), channel_id=1, source_target_pairs={{0,4},{1,5},{2,6},{3,7},{8,12},{9,13},{10,14},{11,15},{16,20},{17,... | collective-permute-start | bytes 322568 | tf_op jit(solution)/shard_map/ppermute | solution.py:19
  18.1 1.3 collective-permute-start.3
  20.7 4.4 %collective-permute-done.3 = bf16[70,3,256]{2,1,0:T(4,128)(2,1)S(1)} collective-permute-done((bf16[70,3,256]{2,1,0:T(4,128)(2,1)S(1)}, bf16[70,3,256]{2,1,0:T(4,128)(2,1)S(1)}, u32[]{:S(2)}, u32[]{:S(2)}) %collective-permute-start.3) | collective-permute-done | bytes 107552 | tf_op jit(solution)/shard_map/ppermute | solution.py:21
  25.7 16.5 %fusion.61 = (f32[64,32]{1,0:T(8,128)S(1)}, f32[64,32,256]{2,1,0:T(8,128)S(1)}) fusion(f32[256]{0:T(256)} %bitcast.192, f32[70,38,256]{2,1,0:T(8,128)S(1)} %maximum_convert_fusion, f32[256]{0:T(256)} %bitcast.193, f32[256]{0:T(256)S(1)} %bitcast.146, f32[256]{0:T(256)S(1)} %bitcast.147, f32[256]{0:T(256)S(1)} %bitcast.148, f32[256]{0:T(256)S(1)} %bitcast.149, ...), kind=kLoop, calls=%fused_computation.170 | loop fusion | flops 51902464 | bytes 104916992 | tf_op jit(solution)/shard_map/reduce_sum | solution.py:154
  43.2 1.7 collective-permute-start.5
  44.9 1.9 collective-permute-start.6
  46.8 2.7 %dynamic-slice_dynamic-update-slice_fusion = (bf16[2048,1024]{1,0:T(8,128)(2,1)}, bf16[2048,1024]{1,0:T(8,128)(2,1)}) fusion(bf16[1024,1024]{1,0:T(8,128)(2,1)S(1)} %copy-done.2, s32[]{:T(128)S(6)} %select_n.4, bf16[1024,1024]{1,0:T(8,128)(2,1)} %param.15), kind=kLoop, calls=%fused_computation.106 | loop fusion | bytes 4194308
  51.4 1.5 add_convert_fusion.2
  52.9 4.6 %all-to-all-start = ((bf16[4,512,256]{2,1,0:T(8,128)(2,1)}), bf16[4,512,256]{2,1,0:T(8,128)(2,1)S(1)}, u32[]{:S(2)}, u32[]{:S(2)}) async-start(bf16[4,512,256]{2,1,0:T(8,128)(2,1)} %bitcast.57), calls=%async_computation | async-start | bytes 2097152 | tf_op jit(solution)/shard_map/all_to_all | solution.py:168
  58.4 10.3 %collective-permute-start.10 = (bf16[272,1024]{1,0:T(8,128)(2,1)}, bf16[272,1024]{1,0:T(8,128)(2,1)S(1)}, u32[]{:S(2)}, u32[]{:S(2)}) collective-permute-start(bf16[272,1024]{1,0:T(8,128)(2,1)} %collective-permute-done.8), channel_id=1, source_target_pairs={{0,16},{4,20},{16,0},{20,4},{1,17},{5,21},{17,1},{21,5},{2,18},{6,... | collective-permute-start | bytes 1671176 | tf_op jit(solution)/shard_map/ppermute | solution.py:66
  68.7 1.4 collective-permute-start.11
  71.4 1.9 slice_dynamic-update-slice_fusion.11
  73.2 1.5 collective-permute-start.14
  75.5 8.4 %collective-permute-start.15 = (bf16[272,1024]{1,0:T(8,128)(2,1)}, bf16[272,1024]{1,0:T(8,128)(2,1)S(1)}, u32[]{:S(2)}, u32[]{:S(2)}) collective-permute-start(bf16[272,1024]{1,0:T(8,128)(2,1)} %collective-permute-done.12), channel_id=1, source_target_pairs={{0,20},{4,16},{16,4},{20,0},{1,21},{5,17},{17,5},{21,1},{2,22},{6,... | collective-permute-start | bytes 1671176 | tf_op jit(solution)/shard_map/ppermute | solution.py:66
  84.7 9.4 %collective-permute-done.10 = bf16[272,1024]{1,0:T(8,128)(2,1)S(1)} collective-permute-done((bf16[272,1024]{1,0:T(8,128)(2,1)}, bf16[272,1024]{1,0:T(8,128)(2,1)S(1)}, u32[]{:S(2)}, u32[]{:S(2)}) %collective-permute-start.10) | collective-permute-done | bytes 557088 | tf_op jit(solution)/shard_map/ppermute | solution.py:66
  94.1 2.3 %collective-permute-start.17 = (bf16[272,1024]{1,0:T(8,128)(2,1)}, bf16[272,1024]{1,0:T(8,128)(2,1)S(1)}, u32[]{:S(2)}, u32[]{:S(2)}) collective-permute-start(bf16[272,1024]{1,0:T(8,128)(2,1)} %collective-permute-done.16), channel_id=1, source_target_pairs={{0,4},{4,0},{16,20},{20,16},{1,5},{5,1},{17,21},{21,17},{2,6},{6,2... | collective-permute-start | bytes 1671176 | tf_op jit(solution)/shard_map/ppermute | solution.py:66
  98.0 9.8 %collective-permute-start.19 = (bf16[272,1024]{1,0:T(8,128)(2,1)}, bf16[272,1024]{1,0:T(8,128)(2,1)}, u32[]{:S(2)}, u32[]{:S(2)}) collective-permute-start(bf16[272,1024]{1,0:T(8,128)(2,1)} %collective-permute-done.16), channel_id=1, source_target_pairs={{0,20},{4,16},{16,4},{20,0},{1,21},{5,17},{17,5},{21,1},{2,22},{6,... | collective-permute-start | bytes 1671176 | tf_op jit(solution)/shard_map/ppermute | solution.py:66
  107.8 10.5 %collective-permute-done.14 = bf16[272,1024]{1,0:T(8,128)(2,1)S(1)} collective-permute-done((bf16[272,1024]{1,0:T(8,128)(2,1)}, bf16[272,1024]{1,0:T(8,128)(2,1)S(1)}, u32[]{:S(2)}, u32[]{:S(2)}) %collective-permute-start.14) | collective-permute-done | bytes 557088 | tf_op jit(solution)/shard_map/ppermute | solution.py:66
  119.1 2.8 %collective-permute-done.17 = bf16[272,1024]{1,0:T(8,128)(2,1)S(1)} collective-permute-done((bf16[272,1024]{1,0:T(8,128)(2,1)}, bf16[272,1024]{1,0:T(8,128)(2,1)S(1)}, u32[]{:S(2)}, u32[]{:S(2)}) %collective-permute-start.17) | collective-permute-done | bytes 557088 | tf_op jit(solution)/shard_map/ppermute | solution.py:66
  121.9 1.9 slice_dynamic-update-slice_fusion.7
  124.6 8.5 %collective-permute-done.18 = bf16[272,1024]{1,0:T(8,128)(2,1)S(1)} collective-permute-done((bf16[272,1024]{1,0:T(8,128)(2,1)}, bf16[272,1024]{1,0:T(8,128)(2,1)S(1)}, u32[]{:S(2)}, u32[]{:S(2)}) %collective-permute-start.18) | collective-permute-done | bytes 557088 | tf_op jit(solution)/shard_map/ppermute | solution.py:66
  137.7 1.9 slice_dynamic-update-slice_fusion.3
  141.3 1.9 slice_dynamic-update-slice_fusion
  143.2 11.9 %shard_map.100 = (f32[512,1024]{1,0:T(8,128)S(1)}, bf16[512,1024]{1,0:T(8,128)(2,1)S(1)}) custom-call(bf16[512,1024]{1,0:T(8,128)(2,1)S(1)} %bitcast.139, bf16[512,1024]{1,0:T(8,128)(2,1)S(1)} %collective-permute-done.7.peer_ref, bf16[2048,1024]{1,0:T(8,128)(2,1)} %get-tuple-element.18.first_ref, bf16[1,2048]{1,0:T(2,128)(2,1)S(1)} %broadcast_in_dim.5.bias_ref, ...), custom_call_target="tpu_custom_call" | custom-call | flops 8589934592 | bytes 8388608 | tf_op jit(solution)/shard_map/pallas_call | solution.py:115
  155.7 2.3 %collective-permute-done.20 = bf16[512,1024]{1,0:T(8,128)(2,1)S(1)} collective-permute-done((bf16[512,1024]{1,0:T(8,128)(2,1)S(1)}, bf16[512,1024]{1,0:T(8,128)(2,1)S(1)}, u32[]{:S(2)}, u32[]{:S(2)}) %collective-permute-start.20) | collective-permute-done | bytes 1048608 | tf_op jit(solution)/shard_map/ppermute | solution.py:172
  158.4 30.7 %all_to_all.32 = bf16[512,4,256]{2,0,1:T(8,128)(2,1)S(1)} all-to-all(bf16[512,4,256]{2,0,1:T(8,128)(2,1)S(1)} %bitcast.142), channel_id=1, replica_groups=mesh['y'=2,'core'=2,'col'=2,'blk'=4] {'blk'}, dimensions={1} | all-to-all | bytes 2097152 | tf_op jit(solution)/shard_map/all_to_all | solution.py:174
  190.3 1.4 add_convert_fusion
  (96 shorter events, 23.8 us)
Async XLA Ops:
  0.0 8.4 %copy-start = (bf16[64,32,256]{2,1,0:T(8,128)(2,1)S(1)}, bf16[64,32,256]{2,1,0:T(8,128)(2,1)}, u32[]{:S(2)}) copy-start(bf16[64,32,256]{2,1,0:T(8,128)(2,1)} %param.10) | copy-start | bytes 3145732
  0.0 11.0 %copy-start.3 = (f32[7,7,256]{2,1,0:T(8,128)S(1)}, f32[7,7,256]{2,1,0:T(8,128)}, u32[]{:S(2)}) copy-start(f32[7,7,256]{2,1,0:T(8,128)} %param.11) | copy-start | bytes 150532
  2.8 54.7 %collective-permute-start.8 = (bf16[272,1024]{1,0:T(8,128)(2,1)}, bf16[272,1024]{1,0:T(8,128)(2,1)}, u32[]{:S(2)}, u32[]{:S(2)}) collective-permute-start(bf16[272,1024]{1,0:T(8,128)(2,1)} %fusion.50), channel_id=1, source_target_pairs={{0,1},{1,2},{2,3},{3,0},{4,5},{5,6},{6,7},{7,4},{8,9},{9,10},{10,1... | collective-permute-start | bytes 1671176 | tf_op jit(solution)/shard_map/ppermute | solution.py:30
  5.8 64.3 %collective-permute-start.12 = (bf16[272,1024]{1,0:T(8,128)(2,1)}, bf16[272,1024]{1,0:T(8,128)(2,1)}, u32[]{:S(2)}, u32[]{:S(2)}) collective-permute-start(bf16[272,1024]{1,0:T(8,128)(2,1)} %fusion.50), channel_id=1, source_target_pairs={{0,2},{1,3},{2,0},{3,1},{4,6},{5,7},{6,4},{7,5},{8,10},{9,11},{10,... | collective-permute-start | bytes 1671176 | tf_op jit(solution)/shard_map/ppermute | solution.py:30
  8.4 3.2 %collective-permute-start = (bf16[3,32,256]{2,1,0:T(8,128)(2,1)S(1)}, bf16[3,32,256]{2,1,0:T(8,128)(2,1)S(1)}, u32[]{:S(2)}, u32[]{:S(2)}) collective-permute-start(bf16[3,32,256]{2,1,0:T(8,128)(2,1)S(1)} %get-tuple-element.16), channel_id=1, source_target_pairs={{0,8},{8,16},{16,24},{1,9},{9,17},{17,25},{2,10},{10,18},{18,26},{... | collective-permute-start | bytes 147464 | tf_op jit(solution)/shard_map/ppermute | solution.py:19
  9.7 4.9 %collective-permute-start.1 = (bf16[3,32,256]{2,1,0:T(8,128)(2,1)S(1)}, bf16[3,32,256]{2,1,0:T(8,128)(2,1)S(1)}, u32[]{:S(2)}, u32[]{:S(2)}) collective-permute-start(bf16[3,32,256]{2,1,0:T(8,128)(2,1)S(1)} %get-tuple-element.15), channel_id=1, source_target_pairs={{8,0},{16,8},{24,16},{9,1},{17,9},{25,17},{10,2},{18,10},{26,18},{... | collective-permute-start | bytes 147464 | tf_op jit(solution)/shard_map/ppermute | solution.py:21
  14.7 6.0 %collective-permute-start.2 = (bf16[70,3,256]{2,1,0:T(4,128)(2,1)S(1)}, bf16[70,3,256]{2,1,0:T(4,128)(2,1)S(1)}, u32[]{:S(2)}, u32[]{:S(2)}) collective-permute-start(bf16[70,3,256]{2,1,0:T(4,128)(2,1)S(1)} %get-tuple-element.13), channel_id=1, source_target_pairs={{0,4},{1,5},{2,6},{3,7},{8,12},{9,13},{10,14},{11,15},{16,20},{17,... | collective-permute-start | bytes 322568 | tf_op jit(solution)/shard_map/ppermute | solution.py:19
  18.1 7.0 %collective-permute-start.3 = (bf16[70,3,256]{2,1,0:T(4,128)(2,1)S(1)}, bf16[70,3,256]{2,1,0:T(4,128)(2,1)S(1)}, u32[]{:S(2)}, u32[]{:S(2)}) collective-permute-start(bf16[70,3,256]{2,1,0:T(4,128)(2,1)S(1)} %get-tuple-element.14), channel_id=1, source_target_pairs={{4,0},{5,1},{6,2},{7,3},{12,8},{13,9},{14,10},{15,11},{20,16},{21,... | collective-permute-start | bytes 322568 | tf_op jit(solution)/shard_map/ppermute | solution.py:21
  42.2 4.6 %copy-start.2 = (bf16[1024,1024]{1,0:T(8,128)(2,1)S(1)}, bf16[1024,1024]{1,0:T(8,128)(2,1)}, u32[]{:S(2)}) copy-start(bf16[1024,1024]{1,0:T(8,128)(2,1)} %param.17) | copy-start | bytes 6291460
  42.9 6.6 %copy-start.8 = (bf16[1024]{0:T(1024)(128)(2,1)S(1)}, bf16[1024]{0:T(1024)(128)(2,1)}, u32[]{:S(2)}) copy-start(bf16[1024]{0:T(1024)(128)(2,1)} %param.16) | copy-start | bytes 6148
  42.9 8.4 %copy-start.4 = (f32[256]{0:T(256)S(1)}, f32[256]{0:T(256)}, u32[]{:S(2)}) copy-start(f32[256]{0:T(256)} %param.14) | copy-start | bytes 3076
  42.9 8.4 %copy-start.5 = (f32[256]{0:T(256)S(1)}, f32[256]{0:T(256)}, u32[]{:S(2)}) copy-start(f32[256]{0:T(256)} %param.13) | copy-start | bytes 3076
  43.0 6.9 %collective-permute-start.4 = (f32[2,64,32]{2,1,0:T(8,128)S(1)}, f32[2,64,32]{2,1,0:T(8,128)S(1)}, u32[]{:S(2)}, u32[]{:S(2)}) collective-permute-start(f32[2,64,32]{2,1,0:T(8,128)S(1)} %pad_maximum_fusion), channel_id=1, source_target_pairs={{0,1},{1,2},{2,3},{3,0},{4,5},{5,6},{6,7},{7,4},{8,9},{9,10},{10,1... | collective-permute-start | bytes 49160 | tf_op jit(solution)/shard_map/ppermute | solution.py:30
  43.2 7.4 %collective-permute-start.5 = (f32[2,64,32]{2,1,0:T(8,128)S(1)}, f32[2,64,32]{2,1,0:T(8,128)S(1)}, u32[]{:S(2)}, u32[]{:S(2)}) collective-permute-start(f32[2,64,32]{2,1,0:T(8,128)S(1)} %pad_maximum_fusion), channel_id=1, source_target_pairs={{0,2},{1,3},{2,0},{3,1},{4,6},{5,7},{6,4},{7,5},{8,10},{9,11},{10,... | collective-permute-start | bytes 49160 | tf_op jit(solution)/shard_map/ppermute | solution.py:30
  44.9 6.4 %collective-permute-start.6 = (f32[2,64,32]{2,1,0:T(8,128)S(1)}, f32[2,64,32]{2,1,0:T(8,128)S(1)}, u32[]{:S(2)}, u32[]{:S(2)}) collective-permute-start(f32[2,64,32]{2,1,0:T(8,128)S(1)} %pad_maximum_fusion), channel_id=1, source_target_pairs={{0,3},{1,0},{2,1},{3,2},{4,7},{5,4},{6,5},{7,6},{8,11},{9,8},{10,9... | collective-permute-start | bytes 49160 | tf_op jit(solution)/shard_map/ppermute | solution.py:30
  49.8 23.4 %collective-permute-start.16 = (bf16[272,1024]{1,0:T(8,128)(2,1)}, bf16[272,1024]{1,0:T(8,128)(2,1)}, u32[]{:S(2)}, u32[]{:S(2)}) collective-permute-start(bf16[272,1024]{1,0:T(8,128)(2,1)} %fusion.50), channel_id=1, source_target_pairs={{0,3},{1,0},{2,1},{3,2},{4,7},{5,4},{6,5},{7,6},{8,11},{9,8},{10,9... | collective-permute-start | bytes 1671176 | tf_op jit(solution)/shard_map/ppermute | solution.py:30
  52.9 81.8 %all-to-all-start = ((bf16[4,512,256]{2,1,0:T(8,128)(2,1)}), bf16[4,512,256]{2,1,0:T(8,128)(2,1)S(1)}, u32[]{:S(2)}, u32[]{:S(2)}) async-start(bf16[4,512,256]{2,1,0:T(8,128)(2,1)} %bitcast.57), calls=%async_computation | async-start | bytes 2097152 | tf_op jit(solution)/shard_map/all_to_all | solution.py:168
  58.4 17.1 %collective-permute-start.9 = (bf16[272,1024]{1,0:T(8,128)(2,1)}, bf16[272,1024]{1,0:T(8,128)(2,1)S(1)}, u32[]{:S(2)}, u32[]{:S(2)}) collective-permute-start(bf16[272,1024]{1,0:T(8,128)(2,1)} %collective-permute-done.8), channel_id=1, source_target_pairs={{0,4},{4,0},{16,20},{20,16},{1,5},{5,1},{17,21},{21,17},{2,6},{6,2... | collective-permute-start | bytes 1671176 | tf_op jit(solution)/shard_map/ppermute | solution.py:66
  58.4 35.7 %collective-permute-start.10 = (bf16[272,1024]{1,0:T(8,128)(2,1)}, bf16[272,1024]{1,0:T(8,128)(2,1)S(1)}, u32[]{:S(2)}, u32[]{:S(2)}) collective-permute-start(bf16[272,1024]{1,0:T(8,128)(2,1)} %collective-permute-done.8), channel_id=1, source_target_pairs={{0,16},{4,20},{16,0},{20,4},{1,17},{5,21},{17,1},{21,5},{2,18},{6,... | collective-permute-start | bytes 1671176 | tf_op jit(solution)/shard_map/ppermute | solution.py:66
  68.7 27.7 %collective-permute-start.11 = (bf16[272,1024]{1,0:T(8,128)(2,1)}, bf16[272,1024]{1,0:T(8,128)(2,1)S(1)}, u32[]{:S(2)}, u32[]{:S(2)}) collective-permute-start(bf16[272,1024]{1,0:T(8,128)(2,1)} %collective-permute-done.8), channel_id=1, source_target_pairs={{0,20},{4,16},{16,4},{20,0},{1,21},{5,17},{17,5},{21,1},{2,22},{6,... | collective-permute-start | bytes 1671176 | tf_op jit(solution)/shard_map/ppermute | solution.py:66
  70.1 27.9 %collective-permute-start.13 = (bf16[272,1024]{1,0:T(8,128)(2,1)}, bf16[272,1024]{1,0:T(8,128)(2,1)S(1)}, u32[]{:S(2)}, u32[]{:S(2)}) collective-permute-start(bf16[272,1024]{1,0:T(8,128)(2,1)} %collective-permute-done.12), channel_id=1, source_target_pairs={{0,4},{4,0},{16,20},{20,16},{1,5},{5,1},{17,21},{21,17},{2,6},{6,2... | collective-permute-start | bytes 1671176 | tf_op jit(solution)/shard_map/ppermute | solution.py:66
  73.2 45.0 %collective-permute-start.14 = (bf16[272,1024]{1,0:T(8,128)(2,1)}, bf16[272,1024]{1,0:T(8,128)(2,1)S(1)}, u32[]{:S(2)}, u32[]{:S(2)}) collective-permute-start(bf16[272,1024]{1,0:T(8,128)(2,1)} %collective-permute-done.12), channel_id=1, source_target_pairs={{0,16},{4,20},{16,0},{20,4},{1,17},{5,21},{17,1},{21,5},{2,18},{6,... | collective-permute-start | bytes 1671176 | tf_op jit(solution)/shard_map/ppermute | solution.py:66
  75.5 43.7 %collective-permute-start.15 = (bf16[272,1024]{1,0:T(8,128)(2,1)}, bf16[272,1024]{1,0:T(8,128)(2,1)S(1)}, u32[]{:S(2)}, u32[]{:S(2)}) collective-permute-start(bf16[272,1024]{1,0:T(8,128)(2,1)} %collective-permute-done.12), channel_id=1, source_target_pairs={{0,20},{4,16},{16,4},{20,0},{1,21},{5,17},{17,5},{21,1},{2,22},{6,... | collective-permute-start | bytes 1671176 | tf_op jit(solution)/shard_map/ppermute | solution.py:66
  94.1 27.8 %collective-permute-start.17 = (bf16[272,1024]{1,0:T(8,128)(2,1)}, bf16[272,1024]{1,0:T(8,128)(2,1)S(1)}, u32[]{:S(2)}, u32[]{:S(2)}) collective-permute-start(bf16[272,1024]{1,0:T(8,128)(2,1)} %collective-permute-done.16), channel_id=1, source_target_pairs={{0,4},{4,0},{16,20},{20,16},{1,5},{5,1},{17,21},{21,17},{2,6},{6,2... | collective-permute-start | bytes 1671176 | tf_op jit(solution)/shard_map/ppermute | solution.py:66
  96.4 36.6 %collective-permute-start.18 = (bf16[272,1024]{1,0:T(8,128)(2,1)}, bf16[272,1024]{1,0:T(8,128)(2,1)S(1)}, u32[]{:S(2)}, u32[]{:S(2)}) collective-permute-start(bf16[272,1024]{1,0:T(8,128)(2,1)} %collective-permute-done.16), channel_id=1, source_target_pairs={{0,16},{4,20},{16,0},{20,4},{1,17},{5,21},{17,1},{21,5},{2,18},{6,... | collective-permute-start | bytes 1671176 | tf_op jit(solution)/shard_map/ppermute | solution.py:66
  98.0 36.9 %collective-permute-start.19 = (bf16[272,1024]{1,0:T(8,128)(2,1)}, bf16[272,1024]{1,0:T(8,128)(2,1)}, u32[]{:S(2)}, u32[]{:S(2)}) collective-permute-start(bf16[272,1024]{1,0:T(8,128)(2,1)} %collective-permute-done.16), channel_id=1, source_target_pairs={{0,20},{4,16},{16,4},{20,0},{1,21},{5,17},{17,5},{21,1},{2,22},{6,... | collective-permute-start | bytes 1671176 | tf_op jit(solution)/shard_map/ppermute | solution.py:66
  134.8 8.4 %collective-permute-start.7 = (bf16[512,1024]{1,0:T(8,128)(2,1)S(1)}, bf16[512,1024]{1,0:T(8,128)(2,1)S(1)}, u32[]{:S(2)}, u32[]{:S(2)}) collective-permute-start(bf16[512,1024]{1,0:T(8,128)(2,1)S(1)} %bitcast.138), channel_id=1, source_target_pairs={{0,8},{8,0},{1,9},{9,1},{2,10},{10,2},{3,11},{11,3},{4,12},{12,4},... | collective-permute-start | bytes 3145736 | tf_op jit(solution)/shard_map/ppermute | solution.py:170
  155.1 2.8 %collective-permute-start.20 = (bf16[512,1024]{1,0:T(8,128)(2,1)S(1)}, bf16[512,1024]{1,0:T(8,128)(2,1)S(1)}, u32[]{:S(2)}, u32[]{:S(2)}) collective-permute-start(bf16[512,1024]{1,0:T(8,128)(2,1)S(1)} %get-tuple-element.8), channel_id=1, source_target_pairs={{0,8},{8,0},{1,9},{9,1},{2,10},{10,2},{3,11},{11,3},{4,12},{12,4},... | collective-permute-start | bytes 3145736 | tf_op jit(solution)/shard_map/ppermute | solution.py:172
  189.1 1.2 copy-start.1
  189.1 1.2 copy-start.6
  189.1 1.2 copy-start.7
